TPU v7x, 32 devices: a whole 2x2x4 slice. The times are simulated.
32 devices in a mesh: sect: 4 (over x, core), grp: 4 (over z), span: 2 (over y).
Axes of the slice: x: 2, y: 2, z: 4, core: 2. Of those that a mesh axis runs over, the one named last changes fastest.
Arguments:
- grad_out: bfloat16 [320, 8192], P('grp', 'span'), may hold values from -6 to 6
- destination: int32 [320], P('grp'), may hold values from 0 to 319, as said below
- w_down: bfloat16 [5120, 8192], P('sect', 'span'), may hold values from -0.078125 to 0.078125
- pre_act: bfloat16 [320, 5120], P('grp', ('sect', 'span')), may hold values from -6 to 6
- w_up: bfloat16 [5120, 5120], P(None, ('sect', 'span')), may hold values from -0.078125 to 0.078125
- queries: bfloat16 [1280, 1280], P('grp', ('sect', 'span')), may hold values from -16 to 16
- key_states: bfloat16 [1280, 1280], P('grp', ('sect', 'span')), may hold values from -16 to 16
- value_states: bfloat16 [1280, 1280], P('grp', ('sect', 'span')), may hold values from -6 to 6
- lengths: int32 [12], replicated, may hold values from 1 to 80, 320 in all
Outputs:
- grad_queries: bfloat16 [1280, 1280], P('grp', ('sect', 'span'))
- grad_keys: bfloat16 [1280, 1280], P('grp', ('sect', 'span'))
- grad_values: bfloat16 [1280, 1280], P('grp', ('sect', 'span'))
Inputs may be any that keep to these rules, and one draw needn't show every extreme that they name: `destination`: a permutation of the merged tokens; the merged tokens on one index of grp go to exactly 4 indices of grp, exactly 20 to each. `lengths`: an image has 4 patches for each merged token; images lie one after another along the merged tokens.
All inputs are finite; a program needn't handle non-finite values.
Results may differ from a plain program's by a relative error of at most 0.015.
Values may be sent and summed in bfloat16 or wider, within the bound.
No kernel may reach another device: no remote copies, remote signals or barrier semaphores. Data moves between devices by JAX's collectives and lax.ppermute only.
A program may use at most 64 MiB of HBM per device.

v0:
```python
import functools

import jax
import jax.numpy as jnp
from jax import lax
from jax.experimental import pallas as pl
from jax.experimental.pallas import tpu as pltpu
from jax.sharding import PartitionSpec as P

HEAD_DIM = 80
SCALE = HEAD_DIM**-0.5
MIB = 1024 * 1024
VMEM = pltpu.MemorySpace.VMEM
NT = (((1,), (1,)), ((), ()))
NN = (((1,), (0,)), ((), ()))
TN = (((0,), (0,)), ((), ()))


def dot(a, b, dims):
    return lax.dot_general(a, b, dims, preferred_element_type=jnp.float32)


def iota(shape, dim):
    return lax.broadcasted_iota(jnp.int32, shape, dim)


def params(mib):
    return pltpu.CompilerParams(vmem_limit_bytes=mib * MIB)


def in_vmem(count):
    return [pl.BlockSpec(memory_space=VMEM) for _ in range(count)]


def padded_slots(row_count, groups):
    offsets = min(groups, row_count // 2)
    capacity = row_count // offsets
    return capacity, -(-(capacity + 1) // 8) * 8


def one_product(count, slots, hidden):
    return count * slots <= hidden


def down_kernel(groups, spans, capacity, slots, chunks, dest_hbm, rows_hbm, weight_ref, out_ref,
                dest_ref, rows_ref, held, sems, first_sems):
    row_count = rows_ref.shape[0]
    dest_copy = pltpu.make_async_copy(dest_hbm, dest_ref, first_sems.at[0])
    dest_copy.start()
    rows_copy = pltpu.make_async_copy(rows_hbm, rows_ref, first_sems.at[1])
    rows_copy.start()
    hidden = weight_ref.shape[0] // spans
    depth = weight_ref.shape[1] // chunks
    copies = []
    for s in range(spans):
        for c in range(chunks):
            part = (pl.ds(s * hidden, hidden), pl.ds(c * depth, depth))
            copy = pltpu.make_async_copy(weight_ref.at[part], held.at[part], sems.at[s * chunks + c])
            copy.start()
            copies.append(copy)
    dest_copy.wait()
    across = jnp.broadcast_to(dest_ref[...].astype(jnp.float32), (row_count, row_count))
    down = across.T
    group_across = jnp.floor((across + 0.5) * (1.0 / row_count))
    group_down = jnp.floor((down + 0.5) * (1.0 / row_count))
    slot_down = down - group_down * row_count
    same = group_across == group_down
    earlier = iota((row_count, row_count), 0) < iota((row_count, row_count), 1)
    later = iota((row_count, row_count), 1) < iota((row_count, row_count), 0)
    rank_across = jnp.sum(jnp.where(same & earlier, 1.0, 0.0), 0, keepdims=True)
    rank_down = jnp.sum(jnp.where(same & later, 1.0, 0.0), 1, keepdims=True)
    row_of = group_across[:1] * slots + rank_across
    places = iota((groups * slots, row_count), 0).astype(jnp.float32)
    pick = jnp.where(places == row_of, 1.0, 0.0).astype(jnp.bfloat16)
    lane = iota((row_count, hidden), 1).astype(jnp.float32)
    shift = 0.0
    if one_product(groups * spans, slots, hidden):
        device = lax.axis_index("grp") * spans + lax.axis_index("span")
        shift = (device * slots).astype(jnp.float32)
    at_rank = lane == rank_down + shift
    label_row = iota((slots, hidden), 0) == capacity
    labels = []
    for g in range(groups):
        hit = at_rank & (group_down[:, :1] == g)
        labels.append(jnp.sum(jnp.where(hit, slot_down[:, :1] + 1.0, 0.0), 0, keepdims=True) - 1.0)
    rows_copy.wait()
    for s in range(spans):
        total = jnp.zeros((row_count, hidden), jnp.float32)
        for c in range(chunks):
            copies[s * chunks + c].wait()
            part = held[s * hidden : (s + 1) * hidden, c * depth : (c + 1) * depth]
            total = total + dot(rows_ref[:, c * depth : (c + 1) * depth], part, NT)
        moved = dot(pick, total.astype(jnp.bfloat16), NN)
        for g in range(groups):
            piece = jnp.where(label_row, labels[g], moved[g * slots : (g + 1) * slots])
            out_ref[g * spans + s] = piece.astype(jnp.bfloat16)


def down_pieces(dest, rows, weight, groups, spans):
    row_count = rows.shape[0]
    capacity, slots = padded_slots(row_count, groups)
    hidden = weight.shape[0] // spans
    chunks = 4
    return pl.pallas_call(
        functools.partial(down_kernel, groups, spans, capacity, slots, chunks),
        out_shape=jax.ShapeDtypeStruct((groups * spans, slots, hidden), jnp.bfloat16),
        in_specs=[pl.BlockSpec(memory_space=pltpu.MemorySpace.HBM)] * 3,
        out_specs=pl.BlockSpec(memory_space=VMEM),
        scratch_shapes=[
            pltpu.VMEM((1, row_count), jnp.int32),
            pltpu.VMEM(rows.shape, jnp.bfloat16),
            pltpu.VMEM(weight.shape, jnp.bfloat16),
            pltpu.SemaphoreType.DMA((spans * chunks,)),
            pltpu.SemaphoreType.DMA((2,)),
        ],
        compiler_params=params(60),
        name="down_product",
    )(dest.reshape(1, row_count), rows, weight)


def up_kernel(heads, capacity, pieces_ref, pre_ref, weight_ref, out_ref, held, sems):
    row_count, hidden = pre_ref.shape
    count, slots, _ = pieces_ref.shape
    width = weight_ref.shape[0] // (4 * heads)
    copies = []
    for h in range(heads):
        for j in range(4):
            copy = pltpu.make_async_copy(
                weight_ref.at[pl.ds((j * heads + h) * width, width)],
                held.at[h, pl.ds(j * width, width)],
                sems.at[h * 4 + j],
            )
            copy.start()
            copies.append(copy)
    label_at = slice(capacity, capacity + 1)
    if one_product(count, slots, hidden):
        pieces = [pieces_ref[p].astype(jnp.float32) for p in range(count)]
        labels = functools.reduce(jnp.maximum, [x[label_at, : count * slots] for x in pieces])
        row = iota((row_count, count * slots), 0).astype(jnp.float32)
        put = jnp.where(row == labels, 1.0, 0.0).astype(jnp.bfloat16)
        total = dot(put, jnp.concatenate(pieces, 0).astype(jnp.bfloat16), NN)
    else:
        row = iota((row_count, slots), 0).astype(jnp.float32)

        def placed(p, total):
            piece = pieces_ref[p]
            labels = piece.astype(jnp.float32)[label_at, :slots]
            put = jnp.where(row == labels, 1.0, 0.0).astype(jnp.bfloat16)
            return total + dot(put, piece, NN)

        total = lax.fori_loop(0, count, placed, jnp.zeros((row_count, hidden), jnp.float32))
    pre = pre_ref[...].astype(jnp.float32)
    cdf = 0.5 * (1.0 + lax.erf(pre * 0.7071067811865476))
    slope = cdf + pre * jnp.exp(-0.5 * pre * pre) * 0.3989422804014327
    grad_pre = (total * slope).astype(jnp.bfloat16)
    for h in range(heads):
        for j in range(4):
            copies[h * 4 + j].wait()
        out_ref[h] = dot(held[h], grad_pre, NT).T.astype(jnp.bfloat16)


def up_pieces(pieces, pre, weight, heads, capacity):
    width = weight.shape[0] // heads
    return pl.pallas_call(
        functools.partial(up_kernel, heads, capacity),
        out_shape=jax.ShapeDtypeStruct((heads, pre.shape[0], width), jnp.bfloat16),
        in_specs=in_vmem(2) + [pl.BlockSpec(memory_space=pltpu.MemorySpace.HBM)],
        out_specs=pl.BlockSpec(memory_space=VMEM),
        scratch_shapes=[
            pltpu.VMEM((heads, width, weight.shape[1]), jnp.bfloat16),
            pltpu.SemaphoreType.DMA((heads * 4,)),
        ],
        compiler_params=params(60),
        name="up_product",
    )(pieces, pre, weight)


def softmax_kernel(lengths_ref, first_ref, own_ref, before_ref, after_ref, _, own_probs_ref,
                   side_probs_ref, attended_ref, values_ref):
    columns, patches = own_ref.shape[0] // 3, own_ref.shape[1]
    first = first_ref[0, 0]

    def image_of(shape, dim):
        token = iota(shape, dim) // 4 + first

        def step(i, state):
            image, bound = state
            bound = bound + lengths_ref[0, i]
            return image + jnp.where(token >= bound, 1, 0), bound

        start = (jnp.where(token < 0, -1, 0), jnp.int32(0))
        return lax.fori_loop(0, lengths_ref.shape[1], step, start)[0]

    key_image = image_of((3 * patches, 1), 0)
    query_image = image_of((1, 3 * patches), 1)
    blocks = (before_ref, own_ref, after_ref)
    heads = columns // HEAD_DIM
    for h in range(heads):
        q, k, v = [
            [b[t * columns + h * HEAD_DIM : t * columns + (h + 1) * HEAD_DIM] for b in blocks]
            for t in range(3)
        ]
        rows_of = lambda x: x.astype(jnp.float32).T.astype(jnp.bfloat16)
        k_rows = [rows_of(x) for x in k]
        for b in range(3):
            values_ref[h, b * patches : (b + 1) * patches] = rows_of(v[b])
        for qb, keys in ((0, (0, 1)), (1, (0, 1, 2)), (2, (1, 2))):
            scores = []
            image = query_image[:, qb * patches : (qb + 1) * patches]
            for kb in keys:
                same = key_image[kb * patches : (kb + 1) * patches] == image
                scores.append(jnp.where(same, dot(k_rows[kb], q[qb], NN) * SCALE, -jnp.inf))
            tops = [jnp.max(s, 0, keepdims=True) for s in scores]
            top = functools.reduce(jnp.maximum, tops)
            weights = [jnp.exp(s - top) for s in scores]
            over = 1.0 / functools.reduce(jnp.add, [jnp.sum(w, 0, keepdims=True) for w in weights])
            attended = jnp.zeros((HEAD_DIM, patches), jnp.float32)
            for kb, w in zip(keys, weights):
                probs = (w * over).astype(jnp.bfloat16)
                attended = attended + dot(v[kb], probs, NN)
                if qb == 1:
                    own_probs_ref[h, kb * patches : (kb + 1) * patches] = probs
                elif kb == 1:
                    side_probs_ref[h, qb // 2] = probs
            attended_ref[qb, h * HEAD_DIM : (h + 1) * HEAD_DIM] = attended


def softmax_parts(lengths, first, own, before, after, later):
    columns, patches = own.shape[0] // 3, own.shape[1]
    heads = columns // HEAD_DIM
    smem = pl.BlockSpec(memory_space=pltpu.MemorySpace.SMEM)
    return pl.pallas_call(
        softmax_kernel,
        out_shape=(
            jax.ShapeDtypeStruct((heads, 3 * patches, patches), jnp.bfloat16),
            jax.ShapeDtypeStruct((heads, 2, patches, patches), jnp.bfloat16),
            jax.ShapeDtypeStruct((3, columns, patches), jnp.float32),
            jax.ShapeDtypeStruct((heads, 3 * patches, HEAD_DIM), jnp.bfloat16),
        ),
        in_specs=[smem, smem] + in_vmem(3) + [pl.BlockSpec(memory_space=pl.ANY)],
        out_specs=tuple(in_vmem(4)),
        compiler_params=params(32),
        name="softmax_parts",
    )(lengths.reshape(1, -1), first.reshape(1, 1), own, before, after, later)


def gather_kernel(pieces_ref, _, out_ref):
    count, row_count, width = pieces_ref.shape
    total = pieces_ref[0].astype(jnp.float32)
    for p in range(1, count):
        total = total + pieces_ref[p].astype(jnp.float32)
    total = total.astype(jnp.bfloat16)
    columns = width // 4
    patch = iota((row_count, 4 * row_count), 1)
    token = iota((row_count, 4 * row_count), 0)
    result = jnp.zeros((columns, 4 * row_count), jnp.float32)
    for j in range(4):
        put = jnp.where(patch == 4 * token + j, 1.0, 0.0).astype(jnp.bfloat16)
        result = result + dot(total[:, j * columns : (j + 1) * columns], put, TN)
    out_ref[...] = result.astype(jnp.bfloat16)


def gathered(pieces, later):
    _, row_count, width = pieces.shape
    return pl.pallas_call(
        gather_kernel,
        out_shape=jax.ShapeDtypeStruct((width // 4, 4 * row_count), jnp.bfloat16),
        in_specs=in_vmem(1) + [pl.BlockSpec(memory_space=pl.ANY)],
        out_specs=pl.BlockSpec(memory_space=VMEM),
        compiler_params=params(16),
        name="gather_sum",
    )(pieces, later)


def own_kernel(grad_ref, own_ref, before_ref, after_ref, probs_ref, attended_ref, values_ref,
               query_ref, key_ref, value_ref):
    columns, patches = grad_ref.shape
    for h in range(columns // HEAD_DIM):
        cols = slice(h * HEAD_DIM, (h + 1) * HEAD_DIM)
        grad = grad_ref[cols]
        delta = jnp.sum(grad.astype(jnp.float32) * attended_ref[1, cols], 0, keepdims=True)
        total = jnp.zeros((HEAD_DIM, patches), jnp.float32)
        for b, ref in enumerate((before_ref, own_ref, after_ref)):
            rows = slice(b * patches, (b + 1) * patches)
            probs = probs_ref[h, rows]
            slope = dot(values_ref[h, rows], grad, NN)
            scores = (probs.astype(jnp.float32) * (slope - delta)).astype(jnp.bfloat16)
            key = ref[columns + h * HEAD_DIM : columns + (h + 1) * HEAD_DIM]
            total = total + dot(key, scores, NN)
            if b == 1:
                key_ref[cols] = dot(ref[cols], scores, NT)
                value_ref[cols] = dot(grad, probs, NT)
        query_ref[cols] = (total * SCALE).astype(jnp.bfloat16)


def own_terms(grad, own, before, after, probs, attended, values):
    return pl.pallas_call(
        own_kernel,
        out_shape=(
            jax.ShapeDtypeStruct(grad.shape, jnp.bfloat16),
            jax.ShapeDtypeStruct(grad.shape, jnp.float32),
            jax.ShapeDtypeStruct(grad.shape, jnp.float32),
        ),
        in_specs=in_vmem(7),
        out_specs=tuple(in_vmem(3)),
        compiler_params=params(32),
        name="own_terms",
    )(grad, own, before, after, probs, attended, values)


def side_kernel(left_ref, right_ref, before_ref, after_ref, probs_ref, attended_ref, values_ref,
                key_part_ref, value_part_ref, key_ref, value_ref):
    columns, patches = left_ref.shape
    for h in range(columns // HEAD_DIM):
        cols = slice(h * HEAD_DIM, (h + 1) * HEAD_DIM)
        key, value = key_part_ref[cols], value_part_ref[cols]
        for side, (grad_ref, ref) in enumerate(((left_ref, before_ref), (right_ref, after_ref))):
            grad = grad_ref[cols]
            delta = jnp.sum(
                grad.astype(jnp.float32) * attended_ref[2 * side, cols], 0, keepdims=True
            )
            probs = probs_ref[h, side]
            slope = dot(values_ref[h, patches : 2 * patches], grad, NN)
            scores = (probs.astype(jnp.float32) * (slope - delta)).astype(jnp.bfloat16)
            key = key + dot(ref[cols], scores, NT)
            value = value + dot(grad, probs, NT)
        key_ref[cols] = (key * SCALE).astype(jnp.bfloat16)
        value_ref[cols] = value.astype(jnp.bfloat16)


def side_terms(left, right, before, after, probs, attended, values, key_part, value_part):
    shape = jax.ShapeDtypeStruct(left.shape, jnp.bfloat16)
    return pl.pallas_call(
        side_kernel,
        out_shape=(shape, shape),
        in_specs=in_vmem(9),
        out_specs=tuple(in_vmem(2)),
        compiler_params=params(32),
        name="side_terms",
    )(left, right, before, after, probs, attended, values, key_part, value_part)


def from_both_sides(x, axis):
    size = lax.axis_size(axis)
    up = [(i, i + 1) for i in range(size - 1)]
    return (
        lax.ppermute(x, axis, up),
        lax.ppermute(x, axis, [(j, i) for i, j in up]),
    )


def on_device(
    grad_out, destination, w_down, pre_act, w_up, queries, key_states, value_states, lengths
):
    groups = lax.axis_size("grp")
    spans = lax.axis_size("span")
    heads = lax.axis_size(("sect", "span"))
    row_count = grad_out.shape[0]
    capacity, _ = padded_slots(row_count, groups)
    pieces = down_pieces(destination, grad_out, w_down, groups, spans)
    arrived = lax.all_to_all(pieces, ("grp", "span"), split_axis=0, concat_axis=0, tiled=True)
    shares = up_pieces(arrived, pre_act, w_up, heads, capacity)
    shares, queries, key_states, value_states = lax.optimization_barrier(
        (shares, queries, key_states, value_states)
    )
    own = jnp.concatenate([queries.T, key_states.T, value_states.T], 0)
    before, after = from_both_sides(own, "grp")
    first = (lax.axis_index("grp") - 1) * row_count
    own_probs, side_probs, attended, values = softmax_parts(
        lengths, first, own, before, after, shares
    )
    shares = lax.all_to_all(shares, ("sect", "span"), split_axis=0, concat_axis=0, tiled=True)
    grad = gathered(shares, values)
    left, right = from_both_sides(grad, "grp")
    grad_query, key_part, value_part = own_terms(
        grad, own, before, after, own_probs, attended, values
    )
    grad_key, grad_value = side_terms(
        left, right, before, after, side_probs, attended, values, key_part, value_part
    )
    return grad_query.T, grad_key.T, grad_value.T


def solution(mesh):
    split = P("grp", ("sect", "span"))
    placed = (
        P("grp", "span"),
        P("grp"),
        P("sect", "span"),
        split,
        P(None, ("sect", "span")),
        split,
        split,
        split,
        P(),
    )
    return jax.shard_map(
        on_device,
        mesh=mesh,
        in_specs=placed,
        out_specs=(split, split, split),
        check_vma=False,
    )
```

profile of v0, /device:TPU:0, one launch (start us, length us, event | category | flops | bytes accessed | tf_op | source)
XLA Modules:
  0.0 76.7 jit_solution(10336624795390840244)
XLA Ops:
  0.6 10.0 %down_product.1 = bf16[8,24,640]{2,1,0:T(8,128)(2,1)} custom-call(s32[1,80]{1,0:T(1,128)} %bitcast.13, bf16[80,4096]{1,0:T(8,128)(2,1)} %rows_hbm.1, bf16[1280,4096]{1,0:T(8,128)(2,1)} %weight_ref.2), custom_call_target="tpu_custom_call" | custom-call | tf_op jit(solution)/shard_map/down_product/pallas_call | solution.py:104
  10.7 0.0 copy-start.6
  10.7 0.0 copy-start.7
  10.7 0.0 copy-start.8
  10.7 0.0 copy-start.5
  10.7 16.2 %all_to_all.10.pieces_ref = bf16[8,24,640]{2,1,0:T(8,128)(2,1)} all-to-all(bf16[8,24,640]{2,1,0:T(8,128)(2,1)} %down_product.1), channel_id=1, replica_groups=mesh['sect'=4,'grp'=4,'span'=2] {'grp','span'}, dimensions={0} | all-to-all | bytes 491520 | tf_op jit(solution)/shard_map/all_to_all | solution.py:361
  26.9 7.7 %up_product.1._ = bf16[8,80,640]{2,1,0:T(8,128)(2,1)} custom-call(bf16[8,24,640]{2,1,0:T(8,128)(2,1)} %all_to_all.10.pieces_ref, bf16[80,640]{1,0:T(8,128)(2,1)} %pre_ref.1, bf16[5120,640]{1,0:T(8,128)(2,1)} %weight_ref.3), custom_call_target="tpu_custom_call" | custom-call | tf_op jit(solution)/shard_map/up_product/pallas_call | solution.py:164
  34.7 3.6 %all-to-all-start.1 = ((bf16[8,80,640]{2,1,0:T(8,128)(2,1)}), bf16[8,80,640]{2,1,0:T(8,128)(2,1)S(1)}, u32[]{:S(2)}, u32[]{:S(2)}) async-start(bf16[8,80,640]{2,1,0:T(8,128)(2,1)} %up_product.1._), calls=%async_computation.1 | async-start | bytes 1638400 | tf_op jit(solution)/shard_map/all_to_all | solution.py:372
  38.2 0.0 copy-done.6
  38.2 0.0 copy-done.7
  38.2 0.0 copy-done.8
  38.3 1.3 %collective-permute-start.1 = (bf16[480,320]{1,0:T(8,128)(2,1)S(1)}, bf16[480,320]{1,0:T(8,128)(2,1)S(1)}, u32[]{:S(2)}, u32[]{:S(2)}) collective-permute-start(bf16[480,320]{1,0:T(8,128)(2,1)S(1)} %pad_maximum_fusion.own_ref), channel_id=1, source_target_pairs={{2,0},{4,2},{6,4},{3,1},{5,3},{7,5},{10,8},{12,10},{14,12},{11,9},... | collective-permute-start | bytes 921608 | tf_op jit(solution)/shard_map/ppermute | solution.py:348
  39.6 4.6 %collective-permute-start = (bf16[480,320]{1,0:T(8,128)(2,1)S(1)}, bf16[480,320]{1,0:T(8,128)(2,1)S(1)}, u32[]{:S(2)}, u32[]{:S(2)}) collective-permute-start(bf16[480,320]{1,0:T(8,128)(2,1)S(1)} %pad_maximum_fusion.own_ref), channel_id=1, source_target_pairs={{0,2},{2,4},{4,6},{1,3},{3,5},{5,7},{8,10},{10,12},{12,14},{9,11},... | collective-permute-start | bytes 921608 | tf_op jit(solution)/shard_map/ppermute | solution.py:347
  44.2 6.9 %collective-permute-done.1.after_ref = bf16[480,320]{1,0:T(8,128)(2,1)S(1)} collective-permute-done((bf16[480,320]{1,0:T(8,128)(2,1)S(1)}, bf16[480,320]{1,0:T(8,128)(2,1)S(1)}, u32[]{:S(2)}, u32[]{:S(2)}) %collective-permute-start.1) | collective-permute-done | bytes 307232 | tf_op jit(solution)/shard_map/ppermute | solution.py:348
  51.1 1.2 %collective-permute-done.before_ref = bf16[480,320]{1,0:T(8,128)(2,1)S(1)} collective-permute-done((bf16[480,320]{1,0:T(8,128)(2,1)S(1)}, bf16[480,320]{1,0:T(8,128)(2,1)S(1)}, u32[]{:S(2)}, u32[]{:S(2)}) %collective-permute-start) | collective-permute-done | bytes 307232 | tf_op jit(solution)/shard_map/ppermute | solution.py:347
  52.3 0.0 copy-done.5
  52.3 1.1 %copy-done = bf16[8,80,640]{2,1,0:T(8,128)(2,1)S(1)} copy-done((bf16[8,80,640]{2,1,0:T(8,128)(2,1)S(1)}, bf16[8,80,640]{2,1,0:T(8,128)(2,1)}, u32[]{:S(2)}) %copy-start) | copy-done | bytes 819224
  53.5 7.4 %softmax_parts.1 = (bf16[2,960,320]{2,1,0:T(8,128)(2,1)S(1)}, bf16[2,2,320,320]{3,2,1,0:T(8,128)(2,1)S(1)}, f32[3,160,320]{2,1,0:T(8,128)S(1)}, bf16[2,960,80]{2,1,0:T(8,128)(2,1)S(1)}) custom-call(s32[1,12]{1,0:T(1,128)S(1)} %bitcast.9, s32[1,1]{1,0:T(1,128)} %bitcast.2.first_ref, bf16[480,320]{1,0:T(8,128)(2,1)S(1)} %pad_maximum_fusion.own_ref, ...), custom_call_target="tpu_custom_call" | custom-call | tf_op jit(solution)/shard_map/softmax_parts/pallas_call | solution.py:232
  60.9 0.0 copy-start.1
  60.9 1.1 %copy-done.1 = bf16[2,960,320]{2,1,0:T(8,128)(2,1)} copy-done((bf16[2,960,320]{2,1,0:T(8,128)(2,1)}, bf16[2,960,320]{2,1,0:T(8,128)(2,1)S(1)}, u32[]{:S(2)}) %copy-start.1) | copy-done | bytes 1228824
  62.0 1.0 %copy-done.3 = bf16[2,2,320,320]{3,2,1,0:T(8,128)(2,1)} copy-done((bf16[2,2,320,320]{3,2,1,0:T(8,128)(2,1)}, bf16[2,2,320,320]{3,2,1,0:T(8,128)(2,1)S(1)}, u32[]{:S(2)}) %copy-start.3) | copy-done | bytes 819224
  62.9 0.0 all-to-all-done.1.pieces_ref
  62.9 0.5 gather_sum.1.grad_ref
  63.4 1.3 %collective-permute-start.3 = (bf16[160,320]{1,0:T(8,128)(2,1)S(1)}, bf16[160,320]{1,0:T(8,128)(2,1)S(1)}, u32[]{:S(2)}, u32[]{:S(2)}) collective-permute-start(bf16[160,320]{1,0:T(8,128)(2,1)S(1)} %gather_sum.1.grad_ref), channel_id=1, source_target_pairs={{2,0},{4,2},{6,4},{3,1},{5,3},{7,5},{10,8},{12,10},{14,12},{11,9},... | collective-permute-start | bytes 307208 | tf_op jit(solution)/shard_map/ppermute | solution.py:348
  64.7 5.0 %collective-permute-start.2 = (bf16[160,320]{1,0:T(8,128)(2,1)S(1)}, bf16[160,320]{1,0:T(8,128)(2,1)S(1)}, u32[]{:S(2)}, u32[]{:S(2)}) collective-permute-start(bf16[160,320]{1,0:T(8,128)(2,1)S(1)} %gather_sum.1.grad_ref), channel_id=1, source_target_pairs={{0,2},{2,4},{4,6},{1,3},{3,5},{5,7},{8,10},{10,12},{12,14},{9,11},... | collective-permute-start | bytes 307208 | tf_op jit(solution)/shard_map/ppermute | solution.py:347
  69.8 0.0 copy-start.2
  69.8 1.4 %copy-done.2 = bf16[2,960,320]{2,1,0:T(8,128)(2,1)S(1)} copy-done((bf16[2,960,320]{2,1,0:T(8,128)(2,1)S(1)}, bf16[2,960,320]{2,1,0:T(8,128)(2,1)}, u32[]{:S(2)}) %copy-start.2) | copy-done | bytes 1228824
  71.1 2.3 %own_terms.1 = (bf16[160,320]{1,0:T(8,128)(2,1)}, f32[160,320]{1,0:T(8,128)S(1)}, f32[160,320]{1,0:T(8,128)S(1)}) custom-call(bf16[160,320]{1,0:T(8,128)(2,1)S(1)} %gather_sum.1.grad_ref, bf16[480,320]{1,0:T(8,128)(2,1)S(1)} %pad_maximum_fusion.own_ref, bf16[480,320]{1,0:T(8,128)(2,1)S(1)} %collective-permute-done.before_ref, ...), custom_call_target="tpu_custom_call" | custom-call | tf_op jit(solution)/shard_map/own_terms/pallas_call | solution.py:297
  73.4 0.0 collective-permute-done.3.right_ref
  73.4 0.0 collective-permute-done.2.left_ref
  73.4 1.2 %copy-done.4 = bf16[2,2,320,320]{3,2,1,0:T(8,128)(2,1)S(1)} copy-done((bf16[2,2,320,320]{3,2,1,0:T(8,128)(2,1)S(1)}, bf16[2,2,320,320]{3,2,1,0:T(8,128)(2,1)}, u32[]{:S(2)}) %copy-start.4) | copy-done | bytes 819224
  74.6 2.1 %side_terms.1 = (bf16[160,320]{1,0:T(8,128)(2,1)}, bf16[160,320]{1,0:T(8,128)(2,1)}) custom-call(bf16[160,320]{1,0:T(8,128)(2,1)S(1)} %collective-permute-done.2.left_ref, bf16[160,320]{1,0:T(8,128)(2,1)S(1)} %collective-permute-done.3.right_ref, bf16[480,320]{1,0:T(8,128)(2,1)S(1)} %collective-permute-done.before_ref, ...), custom_call_target="tpu_custom_call" | custom-call | tf_op jit(solution)/shard_map/side_terms/pallas_call | solution.py:333
  (4 shorter events, 0.0 us)
Async XLA Ops:
  10.7 27.6 %copy-start.6 = (bf16[320,160]{0,1:T(8,128)(2,1)S(1)}, bf16[320,160]{0,1:T(8,128)(2,1)}, u32[]{:S(2)}) copy-start(bf16[320,160]{0,1:T(8,128)(2,1)} %param.16) | copy-start | bytes 307204
  10.7 27.6 %copy-start.7 = (bf16[320,160]{0,1:T(8,128)(2,1)S(1)}, bf16[320,160]{0,1:T(8,128)(2,1)}, u32[]{:S(2)}) copy-start(bf16[320,160]{0,1:T(8,128)(2,1)} %param.15) | copy-start | bytes 307204
  10.7 27.6 %copy-start.8 = (bf16[320,160]{0,1:T(8,128)(2,1)S(1)}, bf16[320,160]{0,1:T(8,128)(2,1)}, u32[]{:S(2)}) copy-start(bf16[320,160]{0,1:T(8,128)(2,1)} %param.14) | copy-start | bytes 307204
  10.7 41.6 %copy-start.5 = (s32[12]{0:T(128)S(1)}, s32[12]{0:T(128)}, u32[]{:S(2)}) copy-start(s32[12]{0:T(128)} %param.17) | copy-start | bytes 148
  34.7 28.3 %all-to-all-start.1 = ((bf16[8,80,640]{2,1,0:T(8,128)(2,1)}), bf16[8,80,640]{2,1,0:T(8,128)(2,1)S(1)}, u32[]{:S(2)}, u32[]{:S(2)}) async-start(bf16[8,80,640]{2,1,0:T(8,128)(2,1)} %up_product.1._), calls=%async_computation.1 | async-start | bytes 1638400 | tf_op jit(solution)/shard_map/all_to_all | solution.py:372
  38.3 12.8 %collective-permute-start.1 = (bf16[480,320]{1,0:T(8,128)(2,1)S(1)}, bf16[480,320]{1,0:T(8,128)(2,1)S(1)}, u32[]{:S(2)}, u32[]{:S(2)}) collective-permute-start(bf16[480,320]{1,0:T(8,128)(2,1)S(1)} %pad_maximum_fusion.own_ref), channel_id=1, source_target_pairs={{2,0},{4,2},{6,4},{3,1},{5,3},{7,5},{10,8},{12,10},{14,12},{11,9},... | collective-permute-start | bytes 921608 | tf_op jit(solution)/shard_map/ppermute | solution.py:348
  39.6 12.7 %collective-permute-start = (bf16[480,320]{1,0:T(8,128)(2,1)S(1)}, bf16[480,320]{1,0:T(8,128)(2,1)S(1)}, u32[]{:S(2)}, u32[]{:S(2)}) collective-permute-start(bf16[480,320]{1,0:T(8,128)(2,1)S(1)} %pad_maximum_fusion.own_ref), channel_id=1, source_target_pairs={{0,2},{2,4},{4,6},{1,3},{3,5},{5,7},{8,10},{10,12},{12,14},{9,11},... | collective-permute-start | bytes 921608 | tf_op jit(solution)/shard_map/ppermute | solution.py:347
  52.3 1.1 %copy-start = (bf16[8,80,640]{2,1,0:T(8,128)(2,1)S(1)}, bf16[8,80,640]{2,1,0:T(8,128)(2,1)}, u32[]{:S(2)}) copy-start(bf16[8,80,640]{2,1,0:T(8,128)(2,1)} %up_product.1._) | copy-start | bytes 2457604
  60.9 1.1 %copy-start.1 = (bf16[2,960,320]{2,1,0:T(8,128)(2,1)}, bf16[2,960,320]{2,1,0:T(8,128)(2,1)S(1)}, u32[]{:S(2)}) copy-start(bf16[2,960,320]{2,1,0:T(8,128)(2,1)S(1)} %get-tuple-element.21.probs_ref) | copy-start | bytes 3686404
  62.0 1.0 %copy-start.3 = (bf16[2,2,320,320]{3,2,1,0:T(8,128)(2,1)}, bf16[2,2,320,320]{3,2,1,0:T(8,128)(2,1)S(1)}, u32[]{:S(2)}) copy-start(bf16[2,2,320,320]{3,2,1,0:T(8,128)(2,1)S(1)} %get-tuple-element.24.probs_ref) | copy-start | bytes 2457604
  63.4 10.0 %collective-permute-start.3 = (bf16[160,320]{1,0:T(8,128)(2,1)S(1)}, bf16[160,320]{1,0:T(8,128)(2,1)S(1)}, u32[]{:S(2)}, u32[]{:S(2)}) collective-permute-start(bf16[160,320]{1,0:T(8,128)(2,1)S(1)} %gather_sum.1.grad_ref), channel_id=1, source_target_pairs={{2,0},{4,2},{6,4},{3,1},{5,3},{7,5},{10,8},{12,10},{14,12},{11,9},... | collective-permute-start | bytes 307208 | tf_op jit(solution)/shard_map/ppermute | solution.py:348
  64.7 8.7 %collective-permute-start.2 = (bf16[160,320]{1,0:T(8,128)(2,1)S(1)}, bf16[160,320]{1,0:T(8,128)(2,1)S(1)}, u32[]{:S(2)}, u32[]{:S(2)}) collective-permute-start(bf16[160,320]{1,0:T(8,128)(2,1)S(1)} %gather_sum.1.grad_ref), channel_id=1, source_target_pairs={{0,2},{2,4},{4,6},{1,3},{3,5},{5,7},{8,10},{10,12},{12,14},{9,11},... | collective-permute-start | bytes 307208 | tf_op jit(solution)/shard_map/ppermute | solution.py:347
  69.8 1.4 %copy-start.2 = (bf16[2,960,320]{2,1,0:T(8,128)(2,1)S(1)}, bf16[2,960,320]{2,1,0:T(8,128)(2,1)}, u32[]{:S(2)}) copy-start(bf16[2,960,320]{2,1,0:T(8,128)(2,1)} %copy-done.1) | copy-start | bytes 3686404
  73.4 1.2 %copy-start.4 = (bf16[2,2,320,320]{3,2,1,0:T(8,128)(2,1)S(1)}, bf16[2,2,320,320]{3,2,1,0:T(8,128)(2,1)}, u32[]{:S(2)}) copy-start(bf16[2,2,320,320]{3,2,1,0:T(8,128)(2,1)} %copy-done.3) | copy-start | bytes 2457604
where the time goes:
time: 77.2 us; the launch traced here: 76.7 us
  Pallas kernels  30 us (39%)
  blocking collectives  16.2 us (21%)
  starting transfers between devices  15.7 us (20%)
  waiting for transfers between devices  8.14 us (11%)
  local copies, waits for them, and re-layouts  5.8 us (8%)
  between operations  0.79 us (1%)
    all_to_all x1, blocking collectives, on_device(): lax.all_to_all(pieces, ('grp', 'span'), split_axis=0, concat_axis=0, tile...  16.2 us
    pallas_call x1, Pallas kernels, down_pieces(): pl.pallas_call(functools.partial(down_kernel, groups, spans, capacity, sl...  10 us
    ppermute x2, starting transfers between devices, from_both_sides(): lax.ppermute(x, axis, up)  9.59 us
    pallas_call x1, Pallas kernels, up_pieces(): pl.pallas_call(functools.partial(up_kernel, heads, capacity), out_shape=j...  7.74 us
    pallas_call x1, Pallas kernels, softmax_parts(): pl.pallas_call(softmax_kernel, out_shape=(jax.ShapeDtypeStruct((heads, 3...  7.39 us
    ppermute x2, waiting for transfers between devices, from_both_sides(): lax.ppermute(x, axis, [(j, i) for i, j in up])  6.95 us
    unnamed x18, local copies, waits for them, and re-layouts  5.8 us
    all_to_all x1, starting transfers between devices, on_device(): lax.all_to_all(shares, ('sect', 'span'), split_axis=0, concat_axis=0, til...  3.56 us
  transfers between devices with their start and end apart: 5, of which 2 were waited for; matrix products, arithmetic and copies ran while one was open for 0% of the time, Pallas kernels for 13%

commit v1 on v0

--- a/solution.py
+++ b/solution.py
@@ -32,33 +32,39 @@
     return [pl.BlockSpec(memory_space=VMEM) for _ in range(count)]
 
 
+def in_hbm(count):
+    return [pl.BlockSpec(memory_space=pltpu.MemorySpace.HBM) for _ in range(count)]
+
+
+def fetched(pairs, sems):
+    copies = [pltpu.make_async_copy(a, b, sems.at[i]) for i, (a, b) in enumerate(pairs)]
+    for copy in copies:
+        copy.start()
+    return copies
+
+
 def padded_slots(row_count, groups):
     offsets = min(groups, row_count // 2)
     capacity = row_count // offsets
     return capacity, -(-(capacity + 1) // 8) * 8
 
 
+DONE = jax.ShapeDtypeStruct((8, 128), jnp.float32)
+
+
 def one_product(count, slots, hidden):
     return count * slots <= hidden
 
 
-def down_kernel(groups, spans, capacity, slots, chunks, dest_hbm, rows_hbm, weight_ref, out_ref,
-                dest_ref, rows_ref, held, sems, first_sems):
+def down_kernel(groups, spans, capacity, slots, step, dest_hbm, rows_hbm, weight_ref, out_ref,
+                dest_ref, rows_ref, held, sems):
     row_count = rows_ref.shape[0]
-    dest_copy = pltpu.make_async_copy(dest_hbm, dest_ref, first_sems.at[0])
-    dest_copy.start()
-    rows_copy = pltpu.make_async_copy(rows_hbm, rows_ref, first_sems.at[1])
-    rows_copy.start()
     hidden = weight_ref.shape[0] // spans
-    depth = weight_ref.shape[1] // chunks
-    copies = []
-    for s in range(spans):
-        for c in range(chunks):
-            part = (pl.ds(s * hidden, hidden), pl.ds(c * depth, depth))
-            copy = pltpu.make_async_copy(weight_ref.at[part], held.at[part], sems.at[s * chunks + c])
-            copy.start()
-            copies.append(copy)
-    dest_copy.wait()
+    pairs = [(dest_hbm, dest_ref), (rows_hbm, rows_ref)]
+    for at in range(0, spans * hidden, step):
+        pairs.append((weight_ref.at[pl.ds(at, step)], held.at[pl.ds(at, step)]))
+    copies = fetched(pairs, sems)
+    copies[0].wait()
     across = jnp.broadcast_to(dest_ref[...].astype(jnp.float32), (row_count, row_count))
     down = across.T
     group_across = jnp.floor((across + 0.5) * (1.0 / row_count))
@@ -83,14 +89,14 @@
     for g in range(groups):
         hit = at_rank & (group_down[:, :1] == g)
         labels.append(jnp.sum(jnp.where(hit, slot_down[:, :1] + 1.0, 0.0), 0, keepdims=True) - 1.0)
-    rows_copy.wait()
+    copies[1].wait()
     for s in range(spans):
-        total = jnp.zeros((row_count, hidden), jnp.float32)
-        for c in range(chunks):
-            copies[s * chunks + c].wait()
-            part = held[s * hidden : (s + 1) * hidden, c * depth : (c + 1) * depth]
-            total = total + dot(rows_ref[:, c * depth : (c + 1) * depth], part, NT)
-        moved = dot(pick, total.astype(jnp.bfloat16), NN)
+        total = []
+        for at in range(s * hidden, (s + 1) * hidden, step):
+            copies[2 + at // step].wait()
+            product = dot(held[at : at + step], rows_ref[...], NT)
+            total.append(product.astype(jnp.bfloat16))
+        moved = dot(pick, jnp.concatenate(total, 0), NT)
         for g in range(groups):
             piece = jnp.where(label_row, labels[g], moved[g * slots : (g + 1) * slots])
             out_ref[g * spans + s] = piece.astype(jnp.bfloat16)
@@ -100,18 +106,17 @@
     row_count = rows.shape[0]
     capacity, slots = padded_slots(row_count, groups)
     hidden = weight.shape[0] // spans
-    chunks = 4
-    return pl.pallas_call(
-        functools.partial(down_kernel, groups, spans, capacity, slots, chunks),
+    step = hidden if hidden < 320 else 320
+    return pl.pallas_call(
+        functools.partial(down_kernel, groups, spans, capacity, slots, step),
         out_shape=jax.ShapeDtypeStruct((groups * spans, slots, hidden), jnp.bfloat16),
-        in_specs=[pl.BlockSpec(memory_space=pltpu.MemorySpace.HBM)] * 3,
+        in_specs=in_hbm(3),
         out_specs=pl.BlockSpec(memory_space=VMEM),
         scratch_shapes=[
             pltpu.VMEM((1, row_count), jnp.int32),
             pltpu.VMEM(rows.shape, jnp.bfloat16),
             pltpu.VMEM(weight.shape, jnp.bfloat16),
-            pltpu.SemaphoreType.DMA((spans * chunks,)),
-            pltpu.SemaphoreType.DMA((2,)),
+            pltpu.SemaphoreType.DMA((2 + weight.shape[0] // step,)),
         ],
         compiler_params=params(60),
         name="down_product",
@@ -164,19 +169,23 @@
     return pl.pallas_call(
         functools.partial(up_kernel, heads, capacity),
         out_shape=jax.ShapeDtypeStruct((heads, pre.shape[0], width), jnp.bfloat16),
-        in_specs=in_vmem(2) + [pl.BlockSpec(memory_space=pltpu.MemorySpace.HBM)],
+        in_specs=in_vmem(2) + in_hbm(1),
         out_specs=pl.BlockSpec(memory_space=VMEM),
         scratch_shapes=[
             pltpu.VMEM((heads, width, weight.shape[1]), jnp.bfloat16),
             pltpu.SemaphoreType.DMA((heads * 4,)),
         ],
         compiler_params=params(60),
+        cost_estimate=pl.CostEstimate(
+            flops=8 * pre.shape[0] * weight.size, bytes_accessed=8 * weight.size, transcendentals=0
+        ),
         name="up_product",
     )(pieces, pre, weight)
 
 
-def softmax_kernel(lengths_ref, first_ref, own_ref, before_ref, after_ref, _, own_probs_ref,
-                   side_probs_ref, attended_ref, values_ref):
+def softmax_kernel(lengths_ref, first_ref, own_ref, before_ref, after_ref, own_probs_out,
+                   side_probs_out, attended_out, values_out, done_ref, own_probs_ref,
+                   side_probs_ref, attended_ref, values_ref, sems):
     columns, patches = own_ref.shape[0] // 3, own_ref.shape[1]
     first = first_ref[0, 0]
 
@@ -217,31 +226,53 @@
             attended = jnp.zeros((HEAD_DIM, patches), jnp.float32)
             for kb, w in zip(keys, weights):
                 probs = (w * over).astype(jnp.bfloat16)
-                attended = attended + dot(v[kb], probs, NN)
                 if qb == 1:
                     own_probs_ref[h, kb * patches : (kb + 1) * patches] = probs
-                elif kb == 1:
-                    side_probs_ref[h, qb // 2] = probs
-            attended_ref[qb, h * HEAD_DIM : (h + 1) * HEAD_DIM] = attended
-
-
-def softmax_parts(lengths, first, own, before, after, later):
+                else:
+                    attended = attended + dot(v[kb], probs, NN)
+                    if kb == 1:
+                        side_probs_ref[h, qb // 2] = probs
+            if qb != 1:
+                attended_ref[qb // 2, h * HEAD_DIM : (h + 1) * HEAD_DIM] = attended
+    pairs = (
+        (own_probs_ref, own_probs_out),
+        (side_probs_ref, side_probs_out),
+        (attended_ref, attended_out),
+        (values_ref, values_out),
+    )
+    copies = [pltpu.make_async_copy(a, b, sems.at[i]) for i, (a, b) in enumerate(pairs)]
+    for copy in copies:
+        copy.start()
+    for copy in copies:
+        copy.wait()
+    done_ref[...] = jnp.zeros(done_ref.shape, jnp.float32)
+
+
+def softmax_parts(lengths, first, own, before, after):
     columns, patches = own.shape[0] // 3, own.shape[1]
     heads = columns // HEAD_DIM
     smem = pl.BlockSpec(memory_space=pltpu.MemorySpace.SMEM)
+    shapes = (
+        jax.ShapeDtypeStruct((heads, 3 * patches, patches), jnp.bfloat16),
+        jax.ShapeDtypeStruct((heads, 2, patches, patches), jnp.bfloat16),
+        jax.ShapeDtypeStruct((2, columns, patches), jnp.float32),
+        jax.ShapeDtypeStruct((heads, 3 * patches, HEAD_DIM), jnp.bfloat16),
+    )
     return pl.pallas_call(
         softmax_kernel,
-        out_shape=(
-            jax.ShapeDtypeStruct((heads, 3 * patches, patches), jnp.bfloat16),
-            jax.ShapeDtypeStruct((heads, 2, patches, patches), jnp.bfloat16),
-            jax.ShapeDtypeStruct((3, columns, patches), jnp.float32),
-            jax.ShapeDtypeStruct((heads, 3 * patches, HEAD_DIM), jnp.bfloat16),
+        out_shape=shapes + (DONE,),
+        in_specs=[smem, smem] + in_vmem(3),
+        out_specs=tuple(in_hbm(4) + in_vmem(1)),
+        scratch_shapes=[pltpu.VMEM(x.shape, x.dtype) for x in shapes]
+        + [pltpu.SemaphoreType.DMA((4,))],
+        compiler_params=params(32),
+        cost_estimate=pl.CostEstimate(
+            flops=200 * 9 * heads * patches * patches,
+            bytes_accessed=30 * heads * patches * patches,
+            transcendentals=9 * heads * patches * patches,
         ),
-        in_specs=[smem, smem] + in_vmem(3) + [pl.BlockSpec(memory_space=pl.ANY)],
-        out_specs=tuple(in_vmem(4)),
-        compiler_params=params(32),
         name="softmax_parts",
-    )(lengths.reshape(1, -1), first.reshape(1, 1), own, before, after, later)
+    )(lengths.reshape(1, -1), first.reshape(1, 1), own, before, after)
 
 
 def gather_kernel(pieces_ref, _, out_ref):
@@ -265,35 +296,42 @@
     return pl.pallas_call(
         gather_kernel,
         out_shape=jax.ShapeDtypeStruct((width // 4, 4 * row_count), jnp.bfloat16),
-        in_specs=in_vmem(1) + [pl.BlockSpec(memory_space=pl.ANY)],
+        in_specs=in_vmem(2),
         out_specs=pl.BlockSpec(memory_space=VMEM),
         compiler_params=params(16),
         name="gather_sum",
     )(pieces, later)
 
 
-def own_kernel(grad_ref, own_ref, before_ref, after_ref, probs_ref, attended_ref, values_ref,
-               query_ref, key_ref, value_ref):
+def own_kernel(grad_ref, own_ref, before_ref, after_ref, probs_hbm, values_hbm,
+               query_ref, key_ref, value_ref, probs_ref, values_ref, sems):
     columns, patches = grad_ref.shape
-    for h in range(columns // HEAD_DIM):
+    heads = columns // HEAD_DIM
+    pairs = [(values_hbm, values_ref)]
+    copies = fetched(pairs + [(probs_hbm.at[h], probs_ref.at[h]) for h in range(heads)], sems)
+    blocks = (before_ref, own_ref, after_ref)
+    copies[0].wait()
+    for h in range(heads):
         cols = slice(h * HEAD_DIM, (h + 1) * HEAD_DIM)
         grad = grad_ref[cols]
-        delta = jnp.sum(grad.astype(jnp.float32) * attended_ref[1, cols], 0, keepdims=True)
+        slopes = [dot(values_ref[h, b * patches : (b + 1) * patches], grad, NN) for b in range(3)]
+        copies[1 + h].wait()
+        probs = [probs_ref[h, b * patches : (b + 1) * patches] for b in range(3)]
+        wide = [p.astype(jnp.float32) for p in probs]
+        delta = sum([jnp.sum(p * s, 0, keepdims=True) for p, s in zip(wide, slopes)])
         total = jnp.zeros((HEAD_DIM, patches), jnp.float32)
-        for b, ref in enumerate((before_ref, own_ref, after_ref)):
-            rows = slice(b * patches, (b + 1) * patches)
-            probs = probs_ref[h, rows]
-            slope = dot(values_ref[h, rows], grad, NN)
-            scores = (probs.astype(jnp.float32) * (slope - delta)).astype(jnp.bfloat16)
+        for b, ref in enumerate(blocks):
+            scores = (wide[b] * (slopes[b] - delta)).astype(jnp.bfloat16)
             key = ref[columns + h * HEAD_DIM : columns + (h + 1) * HEAD_DIM]
             total = total + dot(key, scores, NN)
             if b == 1:
                 key_ref[cols] = dot(ref[cols], scores, NT)
-                value_ref[cols] = dot(grad, probs, NT)
+                value_ref[cols] = dot(grad, probs[b], NT)
         query_ref[cols] = (total * SCALE).astype(jnp.bfloat16)
 
 
-def own_terms(grad, own, before, after, probs, attended, values):
+def own_terms(grad, own, before, after, probs, values):
+    heads = probs.shape[0]
     return pl.pallas_call(
         own_kernel,
         out_shape=(
@@ -301,27 +339,43 @@
             jax.ShapeDtypeStruct(grad.shape, jnp.float32),
             jax.ShapeDtypeStruct(grad.shape, jnp.float32),
         ),
-        in_specs=in_vmem(7),
+        in_specs=in_vmem(4) + in_hbm(2),
         out_specs=tuple(in_vmem(3)),
+        scratch_shapes=[
+            pltpu.VMEM(probs.shape, probs.dtype),
+            pltpu.VMEM(values.shape, values.dtype),
+            pltpu.SemaphoreType.DMA((1 + heads,)),
+        ],
         compiler_params=params(32),
         name="own_terms",
-    )(grad, own, before, after, probs, attended, values)
-
-
-def side_kernel(left_ref, right_ref, before_ref, after_ref, probs_ref, attended_ref, values_ref,
-                key_part_ref, value_part_ref, key_ref, value_ref):
+    )(grad, own, before, after, probs, values)
+
+
+def side_kernel(left_ref, right_ref, before_ref, after_ref, probs_hbm, attended_hbm, values_hbm,
+                key_part_ref, value_part_ref, key_ref, value_ref, probs_ref, attended_ref,
+                values_ref, sems):
     columns, patches = left_ref.shape
-    for h in range(columns // HEAD_DIM):
+    heads = columns // HEAD_DIM
+    middle = pl.ds(patches, patches)
+    pairs = [(values_hbm.at[h, middle], values_ref.at[h]) for h in range(heads)]
+    pairs += [(attended_hbm, attended_ref)]
+    pairs += [(probs_hbm.at[h], probs_ref.at[h]) for h in range(heads)]
+    copies = fetched(pairs, sems)
+    for h in range(heads):
         cols = slice(h * HEAD_DIM, (h + 1) * HEAD_DIM)
+        copies[h].wait()
+        grads = (left_ref[cols], right_ref[cols])
+        slopes = [dot(values_ref[h], grad, NN) for grad in grads]
         key, value = key_part_ref[cols], value_part_ref[cols]
-        for side, (grad_ref, ref) in enumerate(((left_ref, before_ref), (right_ref, after_ref))):
-            grad = grad_ref[cols]
-            delta = jnp.sum(
-                grad.astype(jnp.float32) * attended_ref[2 * side, cols], 0, keepdims=True
-            )
+        if h == 0:
+            copies[heads].wait()
+        copies[heads + 1 + h].wait()
+        for side, ref in enumerate((before_ref, after_ref)):
+            grad = grads[side]
+            attended = attended_ref[side, cols]
+            delta = jnp.sum(grad.astype(jnp.float32) * attended, 0, keepdims=True)
             probs = probs_ref[h, side]
-            slope = dot(values_ref[h, patches : 2 * patches], grad, NN)
-            scores = (probs.astype(jnp.float32) * (slope - delta)).astype(jnp.bfloat16)
+            scores = (probs.astype(jnp.float32) * (slopes[side] - delta)).astype(jnp.bfloat16)
             key = key + dot(ref[cols], scores, NT)
             value = value + dot(grad, probs, NT)
         key_ref[cols] = (key * SCALE).astype(jnp.bfloat16)
@@ -330,11 +384,18 @@
 
 def side_terms(left, right, before, after, probs, attended, values, key_part, value_part):
     shape = jax.ShapeDtypeStruct(left.shape, jnp.bfloat16)
+    heads, _, patches, _ = probs.shape
     return pl.pallas_call(
         side_kernel,
         out_shape=(shape, shape),
-        in_specs=in_vmem(9),
+        in_specs=in_vmem(4) + in_hbm(3) + in_vmem(2),
         out_specs=tuple(in_vmem(2)),
+        scratch_shapes=[
+            pltpu.VMEM(probs.shape, probs.dtype),
+            pltpu.VMEM(attended.shape, attended.dtype),
+            pltpu.VMEM((heads, patches, HEAD_DIM), values.dtype),
+            pltpu.SemaphoreType.DMA((1 + 2 * heads,)),
+        ],
         compiler_params=params(32),
         name="side_terms",
     )(left, right, before, after, probs, attended, values, key_part, value_part)
@@ -358,23 +419,21 @@
     row_count = grad_out.shape[0]
     capacity, _ = padded_slots(row_count, groups)
     pieces = down_pieces(destination, grad_out, w_down, groups, spans)
+    pieces, queries, key_states, value_states = lax.optimization_barrier(
+        (pieces, queries, key_states, value_states)
+    )
     arrived = lax.all_to_all(pieces, ("grp", "span"), split_axis=0, concat_axis=0, tiled=True)
-    shares = up_pieces(arrived, pre_act, w_up, heads, capacity)
-    shares, queries, key_states, value_states = lax.optimization_barrier(
-        (shares, queries, key_states, value_states)
-    )
     own = jnp.concatenate([queries.T, key_states.T, value_states.T], 0)
     before, after = from_both_sides(own, "grp")
     first = (lax.axis_index("grp") - 1) * row_count
-    own_probs, side_probs, attended, values = softmax_parts(
-        lengths, first, own, before, after, shares
-    )
+    own_probs, side_probs, attended, values, softmax_done = softmax_parts(
+        lengths, first, own, before, after
+    )
+    shares = up_pieces(arrived, pre_act, w_up, heads, capacity)
     shares = lax.all_to_all(shares, ("sect", "span"), split_axis=0, concat_axis=0, tiled=True)
-    grad = gathered(shares, values)
+    grad = gathered(shares, softmax_done)
     left, right = from_both_sides(grad, "grp")
-    grad_query, key_part, value_part = own_terms(
-        grad, own, before, after, own_probs, attended, values
-    )
+    grad_query, key_part, value_part = own_terms(grad, own, before, after, own_probs, values)
     grad_key, grad_value = side_terms(
         left, right, before, after, side_probs, attended, values, key_part, value_part
     )

time: 77.2 us -> 77.9 us (level)
  Pallas kernels: 30 us -> 31.8 us
  local copies, waits for them, and re-layouts: 5.8 us -> 4.33 us
    pallas_call x2, Pallas kernels: 9.5 us -> 11.1 us  [the longest x1 7.57 us: softmax_parts(): pl.pallas_call(softmax_kernel, out_shape=shapes + (DONE,), in_specs=[smem...]
    unnamed x18 -> x16, local copies, waits for them, and re-layouts: 5.8 us -> 4.33 us
    pallas_call x1, Pallas kernels: 2.27 us -> 3.55 us  [own_terms(): pl.pallas_call(own_kernel, out_shape=(jax.ShapeDtypeStruct(grad.shape, jn...]
    pallas_call x1, Pallas kernels: 10 us -> 8.92 us  [down_pieces(): pl.pallas_call(functools.partial(down_kernel, groups, spans, capacity, sl...]
  transfers between devices with their start and end apart: 5 -> 5, of which waited for: 2 -> 2; matrix products, arithmetic and copies ran while one was open for 0% -> 0% of each run, Pallas kernels for 13% -> 14%
where the time goes in v1:
time: 77.9 us; the launch traced here: 77.4 us
  Pallas kernels  31.8 us (41%)
  blocking collectives  16.2 us (21%)
  starting transfers between devices  15.9 us (20%)
  waiting for transfers between devices  8.14 us (10%)
  local copies, waits for them, and re-layouts  4.33 us (6%)
  between operations  0.98 us (1%)
    all_to_all x1, blocking collectives, on_device(): lax.all_to_all(pieces, ('grp', 'span'), split_axis=0, concat_axis=0, tile...  16.2 us
    ppermute x2, starting transfers between devices, from_both_sides(): lax.ppermute(x, axis, up)  9.77 us
    pallas_call x1, Pallas kernels, down_pieces(): pl.pallas_call(functools.partial(down_kernel, groups, spans, capacity, sl...  8.92 us
    pallas_call x1, Pallas kernels, up_pieces(): pl.pallas_call(functools.partial(up_kernel, heads, capacity), out_shape=j...  7.72 us
    pallas_call x1, Pallas kernels, softmax_parts(): pl.pallas_call(softmax_kernel, out_shape=shapes + (DONE,), in_specs=[smem...  7.57 us
    ppermute x2, waiting for transfers between devices, from_both_sides(): lax.ppermute(x, axis, [(j, i) for i, j in up])  6.95 us
    unnamed x16, local copies, waits for them, and re-layouts  4.33 us
    all_to_all x1, starting transfers between devices, on_device(): lax.all_to_all(shares, ('sect', 'span'), split_axis=0, concat_axis=0, til...  3.56 us
  transfers between devices with their start and end apart: 5, of which 2 were waited for; matrix products, arithmetic and copies ran while one was open for 0% of the time, Pallas kernels for 14%

profile of v1, /device:TPU:0, one launch (start us, length us, event | category | flops | bytes accessed | tf_op | source)
XLA Modules:
  0.0 77.4 jit_solution(7940406537874609262)
XLA Ops:
  0.6 8.9 %down_product.1 = bf16[8,24,640]{2,1,0:T(8,128)(2,1)} custom-call(s32[1,80]{1,0:T(1,128)} %bitcast.13, bf16[80,4096]{1,0:T(8,128)(2,1)} %rows_hbm.1, bf16[1280,4096]{1,0:T(8,128)(2,1)} %weight_ref.2), custom_call_target="tpu_custom_call" | custom-call | tf_op jit(solution)/shard_map/down_product/pallas_call | solution.py:110
  9.6 0.0 copy-start.5
  9.6 0.0 copy-start.6
  9.6 0.0 copy-start.7
  9.6 0.0 copy-start.4
  9.6 16.2 %all_to_all.10.pieces_ref = bf16[8,24,640]{2,1,0:T(8,128)(2,1)} all-to-all(bf16[8,24,640]{2,1,0:T(8,128)(2,1)} %down_product.1), channel_id=1, replica_groups=mesh['sect'=4,'grp'=4,'span'=2] {'grp','span'}, dimensions={0} | all-to-all | bytes 491520 | tf_op jit(solution)/shard_map/all_to_all | solution.py:425
  25.8 7.7 %up_product.1 = bf16[8,80,640]{2,1,0:T(8,128)(2,1)} custom-call(bf16[8,24,640]{2,1,0:T(8,128)(2,1)} %all_to_all.10.pieces_ref, bf16[80,640]{1,0:T(8,128)(2,1)} %pre_ref.1, bf16[5120,640]{1,0:T(8,128)(2,1)} %weight_ref.3), custom_call_target="tpu_custom_call" | custom-call | flops 2097152000 | bytes 26214400 | tf_op jit(solution)/shard_map/up_product/pallas_call | solution.py:169
  33.5 3.6 %all-to-all-start.1 = ((bf16[8,80,640]{2,1,0:T(8,128)(2,1)}), bf16[8,80,640]{2,1,0:T(8,128)(2,1)S(1)}, u32[]{:S(2)}, u32[]{:S(2)}) async-start(bf16[8,80,640]{2,1,0:T(8,128)(2,1)} %up_product.1), calls=%async_computation.1 | async-start | bytes 1638400 | tf_op jit(solution)/shard_map/all_to_all | solution.py:433
  37.1 0.0 copy-done.5
  37.1 0.0 copy-done.6
  37.1 0.0 copy-done.7
  37.2 1.3 %collective-permute-start.1 = (bf16[480,320]{1,0:T(8,128)(2,1)S(1)}, bf16[480,320]{1,0:T(8,128)(2,1)S(1)}, u32[]{:S(2)}, u32[]{:S(2)}) collective-permute-start(bf16[480,320]{1,0:T(8,128)(2,1)S(1)} %pad_maximum_fusion.own_ref), channel_id=1, source_target_pairs={{2,0},{4,2},{6,4},{3,1},{5,3},{7,5},{10,8},{12,10},{14,12},{11,9},... | collective-permute-start | bytes 921608 | tf_op jit(solution)/shard_map/ppermute | solution.py:409
  38.5 4.6 %collective-permute-start = (bf16[480,320]{1,0:T(8,128)(2,1)S(1)}, bf16[480,320]{1,0:T(8,128)(2,1)S(1)}, u32[]{:S(2)}, u32[]{:S(2)}) collective-permute-start(bf16[480,320]{1,0:T(8,128)(2,1)S(1)} %pad_maximum_fusion.own_ref), channel_id=1, source_target_pairs={{0,2},{2,4},{4,6},{1,3},{3,5},{5,7},{8,10},{10,12},{12,14},{9,11},... | collective-permute-start | bytes 921608 | tf_op jit(solution)/shard_map/ppermute | solution.py:408
  43.1 6.9 %collective-permute-done.1.after_ref = bf16[480,320]{1,0:T(8,128)(2,1)S(1)} collective-permute-done((bf16[480,320]{1,0:T(8,128)(2,1)S(1)}, bf16[480,320]{1,0:T(8,128)(2,1)S(1)}, u32[]{:S(2)}, u32[]{:S(2)}) %collective-permute-start.1) | collective-permute-done | bytes 307232 | tf_op jit(solution)/shard_map/ppermute | solution.py:409
  50.0 1.2 %collective-permute-done.before_ref = bf16[480,320]{1,0:T(8,128)(2,1)S(1)} collective-permute-done((bf16[480,320]{1,0:T(8,128)(2,1)S(1)}, bf16[480,320]{1,0:T(8,128)(2,1)S(1)}, u32[]{:S(2)}, u32[]{:S(2)}) %collective-permute-start) | collective-permute-done | bytes 307232 | tf_op jit(solution)/shard_map/ppermute | solution.py:408
  51.2 0.0 copy-done.4
  51.2 7.6 %softmax_parts.1 = (bf16[2,960,320]{2,1,0:T(8,128)(2,1)S(1)}, bf16[2,2,320,320]{3,2,1,0:T(8,128)(2,1)S(1)}, f32[2,160,320]{2,1,0:T(8,128)S(1)}, bf16[2,960,80]{2,1,0:T(8,128)(2,1)S(1)}, f32[8,128]{1,0:T(8,128)S(1)}) custom-call(s32[1,12]{1,0:T(1,128)S(1)} %bitcast.9, s32[1,1]{1,0:T(1,128)} %bitcast.2.first_ref, ...), custom_call_target="tpu_custom_call" | custom-call | flops 368640000 | bytes 6144000 | tf_op jit(solution)/shard_map/softmax_parts/pallas_call | solution.py:261
  58.8 0.0 copy-start
  58.8 1.1 %copy-done = bf16[2,960,320]{2,1,0:T(8,128)(2,1)} copy-done((bf16[2,960,320]{2,1,0:T(8,128)(2,1)}, bf16[2,960,320]{2,1,0:T(8,128)(2,1)S(1)}, u32[]{:S(2)}) %copy-start) | copy-done | bytes 1228824
  59.9 0.8 %copy-done.2 = f32[2,160,320]{2,1,0:T(8,128)} copy-done((f32[2,160,320]{2,1,0:T(8,128)}, f32[2,160,320]{2,1,0:T(8,128)S(1)}, u32[]{:S(2)}) %copy-start.2) | copy-done | bytes 409624
  60.7 0.0 all-to-all-done.1.pieces_ref
  60.7 0.5 gather_sum.1.grad_ref
  61.2 1.3 %collective-permute-start.3 = (bf16[160,320]{1,0:T(8,128)(2,1)S(1)}, bf16[160,320]{1,0:T(8,128)(2,1)S(1)}, u32[]{:S(2)}, u32[]{:S(2)}) collective-permute-start(bf16[160,320]{1,0:T(8,128)(2,1)S(1)} %gather_sum.1.grad_ref), channel_id=1, source_target_pairs={{2,0},{4,2},{6,4},{3,1},{5,3},{7,5},{10,8},{12,10},{14,12},{11,9},... | collective-permute-start | bytes 307208 | tf_op jit(solution)/shard_map/ppermute | solution.py:409
  62.5 5.2 %collective-permute-start.2 = (bf16[160,320]{1,0:T(8,128)(2,1)S(1)}, bf16[160,320]{1,0:T(8,128)(2,1)S(1)}, u32[]{:S(2)}, u32[]{:S(2)}) collective-permute-start(bf16[160,320]{1,0:T(8,128)(2,1)S(1)} %gather_sum.1.grad_ref), channel_id=1, source_target_pairs={{0,2},{2,4},{4,6},{1,3},{3,5},{5,7},{8,10},{10,12},{12,14},{9,11},... | collective-permute-start | bytes 307208 | tf_op jit(solution)/shard_map/ppermute | solution.py:408
  67.7 0.0 copy-start.1
  67.7 1.4 %copy-done.1 = bf16[2,960,320]{2,1,0:T(8,128)(2,1)S(1)} copy-done((bf16[2,960,320]{2,1,0:T(8,128)(2,1)S(1)}, bf16[2,960,320]{2,1,0:T(8,128)(2,1)}, u32[]{:S(2)}) %copy-start.1) | copy-done | bytes 1228824
  69.1 3.6 %own_terms.1 = (bf16[160,320]{1,0:T(8,128)(2,1)}, f32[160,320]{1,0:T(8,128)S(1)}, f32[160,320]{1,0:T(8,128)S(1)}) custom-call(bf16[160,320]{1,0:T(8,128)(2,1)S(1)} %gather_sum.1.grad_ref, bf16[480,320]{1,0:T(8,128)(2,1)S(1)} %pad_maximum_fusion.own_ref, bf16[480,320]{1,0:T(8,128)(2,1)S(1)} %collective-permute-done.before_ref, ...), custom_call_target="tpu_custom_call" | custom-call | tf_op jit(solution)/shard_map/own_terms/pallas_call | solution.py:335
  72.6 0.0 collective-permute-done.3.right_ref
  72.6 0.0 collective-permute-done.2.left_ref
  72.7 0.0 copy-start.3
  72.7 1.0 %copy-done.3 = f32[2,160,320]{2,1,0:T(8,128)S(1)} copy-done((f32[2,160,320]{2,1,0:T(8,128)S(1)}, f32[2,160,320]{2,1,0:T(8,128)}, u32[]{:S(2)}) %copy-start.3) | copy-done | bytes 409624
  73.7 3.5 %side_terms.1 = (bf16[160,320]{1,0:T(8,128)(2,1)}, bf16[160,320]{1,0:T(8,128)(2,1)}) custom-call(bf16[160,320]{1,0:T(8,128)(2,1)S(1)} %collective-permute-done.2.left_ref, bf16[160,320]{1,0:T(8,128)(2,1)S(1)} %collective-permute-done.3.right_ref, bf16[480,320]{1,0:T(8,128)(2,1)S(1)} %collective-permute-done.before_ref, ...), custom_call_target="tpu_custom_call" | custom-call | tf_op jit(solution)/shard_map/side_terms/pallas_call | solution.py:388
  (2 shorter events, 0.0 us)
Async XLA Ops:
  9.6 27.6 %copy-start.5 = (bf16[320,160]{0,1:T(8,128)(2,1)S(1)}, bf16[320,160]{0,1:T(8,128)(2,1)}, u32[]{:S(2)}) copy-start(bf16[320,160]{0,1:T(8,128)(2,1)} %param.16) | copy-start | bytes 307204
  9.6 27.5 %copy-start.6 = (bf16[320,160]{0,1:T(8,128)(2,1)S(1)}, bf16[320,160]{0,1:T(8,128)(2,1)}, u32[]{:S(2)}) copy-start(bf16[320,160]{0,1:T(8,128)(2,1)} %param.15) | copy-start | bytes 307204
  9.6 27.5 %copy-start.7 = (bf16[320,160]{0,1:T(8,128)(2,1)S(1)}, bf16[320,160]{0,1:T(8,128)(2,1)}, u32[]{:S(2)}) copy-start(bf16[320,160]{0,1:T(8,128)(2,1)} %param.14) | copy-start | bytes 307204
  9.6 41.6 %copy-start.4 = (s32[12]{0:T(128)S(1)}, s32[12]{0:T(128)}, u32[]{:S(2)}) copy-start(s32[12]{0:T(128)} %param.17) | copy-start | bytes 148
  33.5 27.2 %all-to-all-start.1 = ((bf16[8,80,640]{2,1,0:T(8,128)(2,1)}), bf16[8,80,640]{2,1,0:T(8,128)(2,1)S(1)}, u32[]{:S(2)}, u32[]{:S(2)}) async-start(bf16[8,80,640]{2,1,0:T(8,128)(2,1)} %up_product.1), calls=%async_computation.1 | async-start | bytes 1638400 | tf_op jit(solution)/shard_map/all_to_all | solution.py:433
  37.2 12.8 %collective-permute-start.1 = (bf16[480,320]{1,0:T(8,128)(2,1)S(1)}, bf16[480,320]{1,0:T(8,128)(2,1)S(1)}, u32[]{:S(2)}, u32[]{:S(2)}) collective-permute-start(bf16[480,320]{1,0:T(8,128)(2,1)S(1)} %pad_maximum_fusion.own_ref), channel_id=1, source_target_pairs={{2,0},{4,2},{6,4},{3,1},{5,3},{7,5},{10,8},{12,10},{14,12},{11,9},... | collective-permute-start | bytes 921608 | tf_op jit(solution)/shard_map/ppermute | solution.py:409
  38.5 12.7 %collective-permute-start = (bf16[480,320]{1,0:T(8,128)(2,1)S(1)}, bf16[480,320]{1,0:T(8,128)(2,1)S(1)}, u32[]{:S(2)}, u32[]{:S(2)}) collective-permute-start(bf16[480,320]{1,0:T(8,128)(2,1)S(1)} %pad_maximum_fusion.own_ref), channel_id=1, source_target_pairs={{0,2},{2,4},{4,6},{1,3},{3,5},{5,7},{8,10},{10,12},{12,14},{9,11},... | collective-permute-start | bytes 921608 | tf_op jit(solution)/shard_map/ppermute | solution.py:408
  58.8 1.1 %copy-start = (bf16[2,960,320]{2,1,0:T(8,128)(2,1)}, bf16[2,960,320]{2,1,0:T(8,128)(2,1)S(1)}, u32[]{:S(2)}) copy-start(bf16[2,960,320]{2,1,0:T(8,128)(2,1)S(1)} %get-tuple-element.22.probs_hbm) | copy-start | bytes 3686404
  59.9 0.8 %copy-start.2 = (f32[2,160,320]{2,1,0:T(8,128)}, f32[2,160,320]{2,1,0:T(8,128)S(1)}, u32[]{:S(2)}) copy-start(f32[2,160,320]{2,1,0:T(8,128)S(1)} %get-tuple-element.26.attended_hbm) | copy-start | bytes 1228804
  61.2 11.4 %collective-permute-start.3 = (bf16[160,320]{1,0:T(8,128)(2,1)S(1)}, bf16[160,320]{1,0:T(8,128)(2,1)S(1)}, u32[]{:S(2)}, u32[]{:S(2)}) collective-permute-start(bf16[160,320]{1,0:T(8,128)(2,1)S(1)} %gather_sum.1.grad_ref), channel_id=1, source_target_pairs={{2,0},{4,2},{6,4},{3,1},{5,3},{7,5},{10,8},{12,10},{14,12},{11,9},... | collective-permute-start | bytes 307208 | tf_op jit(solution)/shard_map/ppermute | solution.py:409
  62.5 10.2 %collective-permute-start.2 = (bf16[160,320]{1,0:T(8,128)(2,1)S(1)}, bf16[160,320]{1,0:T(8,128)(2,1)S(1)}, u32[]{:S(2)}, u32[]{:S(2)}) collective-permute-start(bf16[160,320]{1,0:T(8,128)(2,1)S(1)} %gather_sum.1.grad_ref), channel_id=1, source_target_pairs={{0,2},{2,4},{4,6},{1,3},{3,5},{5,7},{8,10},{10,12},{12,14},{9,11},... | collective-permute-start | bytes 307208 | tf_op jit(solution)/shard_map/ppermute | solution.py:408
  67.7 1.4 %copy-start.1 = (bf16[2,960,320]{2,1,0:T(8,128)(2,1)S(1)}, bf16[2,960,320]{2,1,0:T(8,128)(2,1)}, u32[]{:S(2)}) copy-start(bf16[2,960,320]{2,1,0:T(8,128)(2,1)} %copy-done) | copy-start | bytes 3686404
  72.7 1.0 %copy-start.3 = (f32[2,160,320]{2,1,0:T(8,128)S(1)}, f32[2,160,320]{2,1,0:T(8,128)}, u32[]{:S(2)}) copy-start(f32[2,160,320]{2,1,0:T(8,128)} %copy-done.2) | copy-start | bytes 1228804

commit v2 on v1

--- a/solution.py
+++ b/solution.py
@@ -265,10 +265,10 @@
         out_specs=tuple(in_hbm(4) + in_vmem(1)),
         scratch_shapes=[pltpu.VMEM(x.shape, x.dtype) for x in shapes]
         + [pltpu.SemaphoreType.DMA((4,))],
-        compiler_params=params(32),
+        compiler_params=params(60),
         cost_estimate=pl.CostEstimate(
-            flops=200 * 9 * heads * patches * patches,
-            bytes_accessed=30 * heads * patches * patches,
+            flops=100_000 * heads * patches * patches,
+            bytes_accessed=500 * heads * patches * patches,
             transcendentals=9 * heads * patches * patches,
         ),
         name="softmax_parts",
@@ -303,20 +303,16 @@
     )(pieces, later)
 
 
-def own_kernel(grad_ref, own_ref, before_ref, after_ref, probs_hbm, values_hbm,
-               query_ref, key_ref, value_ref, probs_ref, values_ref, sems):
+def own_kernel(grad_ref, own_ref, before_ref, after_ref, probs_ref, values_ref,
+               query_ref, key_ref, value_ref):
     columns, patches = grad_ref.shape
-    heads = columns // HEAD_DIM
-    pairs = [(values_hbm, values_ref)]
-    copies = fetched(pairs + [(probs_hbm.at[h], probs_ref.at[h]) for h in range(heads)], sems)
     blocks = (before_ref, own_ref, after_ref)
-    copies[0].wait()
-    for h in range(heads):
+    for h in range(columns // HEAD_DIM):
         cols = slice(h * HEAD_DIM, (h + 1) * HEAD_DIM)
         grad = grad_ref[cols]
-        slopes = [dot(values_ref[h, b * patches : (b + 1) * patches], grad, NN) for b in range(3)]
-        copies[1 + h].wait()
-        probs = [probs_ref[h, b * patches : (b + 1) * patches] for b in range(3)]
+        rows = [slice(b * patches, (b + 1) * patches) for b in range(3)]
+        slopes = [dot(values_ref[h, r], grad, NN) for r in rows]
+        probs = [probs_ref[h, r] for r in rows]
         wide = [p.astype(jnp.float32) for p in probs]
         delta = sum([jnp.sum(p * s, 0, keepdims=True) for p, s in zip(wide, slopes)])
         total = jnp.zeros((HEAD_DIM, patches), jnp.float32)
@@ -331,7 +327,6 @@
 
 
 def own_terms(grad, own, before, after, probs, values):
-    heads = probs.shape[0]
     return pl.pallas_call(
         own_kernel,
         out_shape=(
@@ -339,43 +334,26 @@
             jax.ShapeDtypeStruct(grad.shape, jnp.float32),
             jax.ShapeDtypeStruct(grad.shape, jnp.float32),
         ),
-        in_specs=in_vmem(4) + in_hbm(2),
+        in_specs=in_vmem(6),
         out_specs=tuple(in_vmem(3)),
-        scratch_shapes=[
-            pltpu.VMEM(probs.shape, probs.dtype),
-            pltpu.VMEM(values.shape, values.dtype),
-            pltpu.SemaphoreType.DMA((1 + heads,)),
-        ],
         compiler_params=params(32),
         name="own_terms",
     )(grad, own, before, after, probs, values)
 
 
-def side_kernel(left_ref, right_ref, before_ref, after_ref, probs_hbm, attended_hbm, values_hbm,
-                key_part_ref, value_part_ref, key_ref, value_ref, probs_ref, attended_ref,
-                values_ref, sems):
+def side_kernel(left_ref, right_ref, before_ref, after_ref, probs_ref, attended_ref, values_ref,
+                key_part_ref, value_part_ref, key_ref, value_ref):
     columns, patches = left_ref.shape
-    heads = columns // HEAD_DIM
-    middle = pl.ds(patches, patches)
-    pairs = [(values_hbm.at[h, middle], values_ref.at[h]) for h in range(heads)]
-    pairs += [(attended_hbm, attended_ref)]
-    pairs += [(probs_hbm.at[h], probs_ref.at[h]) for h in range(heads)]
-    copies = fetched(pairs, sems)
-    for h in range(heads):
+    for h in range(columns // HEAD_DIM):
         cols = slice(h * HEAD_DIM, (h + 1) * HEAD_DIM)
-        copies[h].wait()
-        grads = (left_ref[cols], right_ref[cols])
-        slopes = [dot(values_ref[h], grad, NN) for grad in grads]
         key, value = key_part_ref[cols], value_part_ref[cols]
-        if h == 0:
-            copies[heads].wait()
-        copies[heads + 1 + h].wait()
-        for side, ref in enumerate((before_ref, after_ref)):
-            grad = grads[side]
+        for side, (grad_ref, ref) in enumerate(((left_ref, before_ref), (right_ref, after_ref))):
+            grad = grad_ref[cols]
             attended = attended_ref[side, cols]
             delta = jnp.sum(grad.astype(jnp.float32) * attended, 0, keepdims=True)
             probs = probs_ref[h, side]
-            scores = (probs.astype(jnp.float32) * (slopes[side] - delta)).astype(jnp.bfloat16)
+            slope = dot(values_ref[h, patches : 2 * patches], grad, NN)
+            scores = (probs.astype(jnp.float32) * (slope - delta)).astype(jnp.bfloat16)
             key = key + dot(ref[cols], scores, NT)
             value = value + dot(grad, probs, NT)
         key_ref[cols] = (key * SCALE).astype(jnp.bfloat16)
@@ -384,18 +362,11 @@
 
 def side_terms(left, right, before, after, probs, attended, values, key_part, value_part):
     shape = jax.ShapeDtypeStruct(left.shape, jnp.bfloat16)
-    heads, _, patches, _ = probs.shape
     return pl.pallas_call(
         side_kernel,
         out_shape=(shape, shape),
-        in_specs=in_vmem(4) + in_hbm(3) + in_vmem(2),
+        in_specs=in_vmem(9),
         out_specs=tuple(in_vmem(2)),
-        scratch_shapes=[
-            pltpu.VMEM(probs.shape, probs.dtype),
-            pltpu.VMEM(attended.shape, attended.dtype),
-            pltpu.VMEM((heads, patches, HEAD_DIM), values.dtype),
-            pltpu.SemaphoreType.DMA((1 + 2 * heads,)),
-        ],
         compiler_params=params(32),
         name="side_terms",
     )(left, right, before, after, probs, attended, values, key_part, value_part)

time: 77.9 us -> 74 us (0.950)
  blocking collectives: 16.2 us -> 0 us
  local copies, waits for them, and re-layouts: 4.33 us -> 12.8 us
  starting transfers between devices: 15.9 us -> 22.7 us
  waiting for transfers between devices: 8.14 us -> 5.63 us
    all_to_all x1 -> x0, blocking collectives: 16.2 us -> none  [on_device(): lax.all_to_all(pieces, ('grp', 'span'), split_axis=0, concat_axis=0, tile...]
    unnamed x16 -> x36, local copies, waits for them, and re-layouts: 4.33 us -> 12.8 us
    all_to_all x0 -> x1, starting transfers between devices: none -> 7.3 us  [on_device(): lax.all_to_all(pieces, ('grp', 'span'), split_axis=0, concat_axis=0, tile...]
    ppermute x2, waiting for transfers between devices: 6.95 us -> 0.01 us  [from_both_sides(): lax.ppermute(x, axis, [(j, i) for i, j in up])]
    all_to_all x0 -> x1, waiting for transfers between devices: none -> 3.85 us  [on_device(): lax.all_to_all(pieces, ('grp', 'span'), split_axis=0, concat_axis=0, tile...]
    pallas_call x1, Pallas kernels: 7.57 us -> 9.38 us  [softmax_parts(): pl.pallas_call(softmax_kernel, out_shape=shapes + (DONE,), in_specs=[smem...]
    all_to_all x1, waiting for transfers between devices: 0.01 us -> 1.77 us  [on_device(): lax.all_to_all(shares, ('sect', 'span'), split_axis=0, concat_axis=0, til...]
    pallas_call x1, Pallas kernels: 3.55 us -> 2.11 us  [side_terms(): pl.pallas_call(side_kernel, out_shape=(shape, shape), in_specs=in_vmem(9)...]
  transfers between devices with their start and end apart: 5 -> 6, of which waited for: 2 -> 2; matrix products, arithmetic and copies ran while one was open for 0% -> 0% of each run, Pallas kernels for 14% -> 27%
where the time goes in v2:
time: 74 us; the launch traced here: 73.2 us
  Pallas kernels  31.1 us (42%)
  starting transfers between devices  22.7 us (31%)
  local copies, waits for them, and re-layouts  12.8 us (17%)
  waiting for transfers between devices  5.63 us (8%)
  between operations  0.83 us (1%)
    unnamed x36, local copies, waits for them, and re-layouts  12.8 us
    pallas_call x1, Pallas kernels, softmax_parts(): pl.pallas_call(softmax_kernel, out_shape=shapes + (DONE,), in_specs=[smem...  9.38 us
    ppermute x2, starting transfers between devices, from_both_sides(): lax.ppermute(x, axis, up)  9.3 us
    pallas_call x1, Pallas kernels, down_pieces(): pl.pallas_call(functools.partial(down_kernel, groups, spans, capacity, sl...  8.95 us
    pallas_call x1, Pallas kernels, up_pieces(): pl.pallas_call(functools.partial(up_kernel, heads, capacity), out_shape=j...  7.72 us
    all_to_all x1, starting transfers between devices, on_device(): lax.all_to_all(pieces, ('grp', 'span'), split_axis=0, concat_axis=0, tile...  7.3 us
    all_to_all x1, waiting for transfers between devices, on_device(): lax.all_to_all(pieces, ('grp', 'span'), split_axis=0, concat_axis=0, tile...  3.85 us
    all_to_all x1, starting transfers between devices, on_device(): lax.all_to_all(shares, ('sect', 'span'), split_axis=0, concat_axis=0, til...  3.56 us
  transfers between devices with their start and end apart: 6, of which 2 were waited for; matrix products, arithmetic and copies ran while one was open for 0% of the time, Pallas kernels for 27%

profile of v2, /device:TPU:0, one launch (start us, length us, event | category | flops | bytes accessed | tf_op | source)
XLA Modules:
  0.0 73.2 jit_solution(18081225030061765646)
XLA Ops:
  0.7 8.9 %down_product.1 = bf16[8,24,640]{2,1,0:T(8,128)(2,1)} custom-call(s32[1,80]{1,0:T(1,128)} %bitcast.12, bf16[80,4096]{1,0:T(8,128)(2,1)} %rows_hbm.1, bf16[1280,4096]{1,0:T(8,128)(2,1)} %weight_ref.2), custom_call_target="tpu_custom_call" | custom-call | tf_op jit(solution)/shard_map/down_product/pallas_call | solution.py:110
  9.6 7.3 %all-to-all-start = ((bf16[8,24,640]{2,1,0:T(8,128)(2,1)}), bf16[8,24,640]{2,1,0:T(8,128)(2,1)S(1)}, u32[]{:S(2)}, u32[]{:S(2)}) async-start(bf16[8,24,640]{2,1,0:T(8,128)(2,1)} %down_product.1), calls=%async_computation | async-start | bytes 491520 | tf_op jit(solution)/shard_map/all_to_all | solution.py:396
  17.0 1.3 %collective-permute-start.1 = (bf16[480,320]{1,0:T(8,128)(2,1)S(1)}, bf16[480,320]{1,0:T(8,128)(2,1)S(1)}, u32[]{:S(2)}, u32[]{:S(2)}) collective-permute-start(bf16[480,320]{1,0:T(8,128)(2,1)S(1)} %pad_maximum_fusion.own_ref), channel_id=1, source_target_pairs={{2,0},{4,2},{6,4},{3,1},{5,3},{7,5},{10,8},{12,10},{14,12},{11,9},... | collective-permute-start | bytes 921608 | tf_op jit(solution)/shard_map/ppermute | solution.py:380
  18.3 4.6 %collective-permute-start = (bf16[480,320]{1,0:T(8,128)(2,1)S(1)}, bf16[480,320]{1,0:T(8,128)(2,1)S(1)}, u32[]{:S(2)}, u32[]{:S(2)}) collective-permute-start(bf16[480,320]{1,0:T(8,128)(2,1)S(1)} %pad_maximum_fusion.own_ref), channel_id=1, source_target_pairs={{0,2},{2,4},{4,6},{1,3},{3,5},{5,7},{8,10},{10,12},{12,14},{9,11},... | collective-permute-start | bytes 921608 | tf_op jit(solution)/shard_map/ppermute | solution.py:379
  22.9 3.9 %all-to-all-done.pieces_ref = bf16[8,24,640]{2,1,0:T(8,128)(2,1)S(1)} async-done(((bf16[8,24,640]{2,1,0:T(8,128)(2,1)}), bf16[8,24,640]{2,1,0:T(8,128)(2,1)S(1)}, u32[]{:S(2)}, u32[]{:S(2)}) %all-to-all-start) | async-done | bytes 245792 | tf_op jit(solution)/shard_map/all_to_all | solution.py:396
  26.7 0.7 copy-done.14
  27.4 7.7 %up_product.1 = bf16[8,80,640]{2,1,0:T(8,128)(2,1)} custom-call(bf16[8,24,640]{2,1,0:T(8,128)(2,1)} %copy-done.14, bf16[80,640]{1,0:T(8,128)(2,1)} %pre_ref.1, bf16[5120,640]{1,0:T(8,128)(2,1)} %weight_ref.3), custom_call_target="tpu_custom_call" | custom-call | flops 2097152000 | bytes 26214400 | tf_op jit(solution)/shard_map/up_product/pallas_call | solution.py:169
  35.2 3.6 %all-to-all-start.1 = ((bf16[8,80,640]{2,1,0:T(8,128)(2,1)}), bf16[8,80,640]{2,1,0:T(8,128)(2,1)S(1)}, u32[]{:S(2)}, u32[]{:S(2)}) async-start(bf16[8,80,640]{2,1,0:T(8,128)(2,1)} %up_product.1), calls=%async_computation.1 | async-start | bytes 1638400 | tf_op jit(solution)/shard_map/all_to_all | solution.py:404
  38.7 0.0 collective-permute-done.1.after_ref
  38.8 0.0 collective-permute-done.before_ref
  38.8 0.7 copy-done.2
  39.5 0.1 copy-done.5
  39.6 9.4 %softmax_parts.1 = (bf16[2,960,320]{2,1,0:T(8,128)(2,1)}, bf16[2,2,320,320]{3,2,1,0:T(8,128)(2,1)}, f32[2,160,320]{2,1,0:T(8,128)}, bf16[2,960,80]{2,1,0:T(8,128)(2,1)}, f32[8,128]{1,0:T(8,128)}) custom-call(s32[1,12]{1,0:T(1,128)} %bitcast.16, s32[1,1]{1,0:T(1,128)} %bitcast.2.first_ref, bf16[480,320]{1,0:T(8,128)(2,1)} %copy-done.8, ...), custom_call_target="tpu_custom_call" | custom-call | flops 20480000000 | bytes 102400000 | tf_op jit(solution)/shard_map/softmax_parts/pallas_call | solution.py:261
  49.0 1.8 %all-to-all-done.1.pieces_ref = bf16[8,80,640]{2,1,0:T(8,128)(2,1)S(1)} async-done(((bf16[8,80,640]{2,1,0:T(8,128)(2,1)}), bf16[8,80,640]{2,1,0:T(8,128)(2,1)S(1)}, u32[]{:S(2)}, u32[]{:S(2)}) %all-to-all-start.1) | async-done | bytes 819232 | tf_op jit(solution)/shard_map/all_to_all | solution.py:404
  50.8 0.7 copy-done.13
  51.5 0.5 gather_sum.1.grad_ref
  51.9 1.3 %collective-permute-start.3 = (bf16[160,320]{1,0:T(8,128)(2,1)S(1)}, bf16[160,320]{1,0:T(8,128)(2,1)S(1)}, u32[]{:S(2)}, u32[]{:S(2)}) collective-permute-start(bf16[160,320]{1,0:T(8,128)(2,1)S(1)} %gather_sum.1.grad_ref), channel_id=1, source_target_pairs={{2,0},{4,2},{6,4},{3,1},{5,3},{7,5},{10,8},{12,10},{14,12},{11,9},... | collective-permute-start | bytes 307208 | tf_op jit(solution)/shard_map/ppermute | solution.py:380
  53.2 4.7 %collective-permute-start.2 = (bf16[160,320]{1,0:T(8,128)(2,1)S(1)}, bf16[160,320]{1,0:T(8,128)(2,1)S(1)}, u32[]{:S(2)}, u32[]{:S(2)}) collective-permute-start(bf16[160,320]{1,0:T(8,128)(2,1)S(1)} %gather_sum.1.grad_ref), channel_id=1, source_target_pairs={{0,2},{2,4},{4,6},{1,3},{3,5},{5,7},{8,10},{10,12},{12,14},{9,11},... | collective-permute-start | bytes 307208 | tf_op jit(solution)/shard_map/ppermute | solution.py:379
  58.0 1.0 %copy-done = bf16[2,960,80]{2,1,0:T(8,128)(2,1)S(1)} copy-done((bf16[2,960,80]{2,1,0:T(8,128)(2,1)S(1)}, bf16[2,960,80]{2,1,0:T(8,128)(2,1)}, u32[]{:S(2)}) %copy-start) | copy-done | bytes 307224
  59.0 1.0 %copy-done.3 = bf16[480,320]{1,0:T(8,128)(2,1)S(1)} copy-done((bf16[480,320]{1,0:T(8,128)(2,1)S(1)}, bf16[480,320]{1,0:T(8,128)(2,1)}, u32[]{:S(2)}) %copy-start.3) | copy-done | bytes 307224
  60.0 1.0 %copy-done.6 = bf16[480,320]{1,0:T(8,128)(2,1)S(1)} copy-done((bf16[480,320]{1,0:T(8,128)(2,1)S(1)}, bf16[480,320]{1,0:T(8,128)(2,1)}, u32[]{:S(2)}) %copy-start.6) | copy-done | bytes 307224
  61.0 1.0 %copy-done.9 = bf16[480,320]{1,0:T(8,128)(2,1)S(1)} copy-done((bf16[480,320]{1,0:T(8,128)(2,1)S(1)}, bf16[480,320]{1,0:T(8,128)(2,1)}, u32[]{:S(2)}) %copy-start.9) | copy-done | bytes 307224
  62.0 1.4 %copy-done.10 = bf16[2,960,320]{2,1,0:T(8,128)(2,1)S(1)} copy-done((bf16[2,960,320]{2,1,0:T(8,128)(2,1)S(1)}, bf16[2,960,320]{2,1,0:T(8,128)(2,1)}, u32[]{:S(2)}) %copy-start.10) | copy-done | bytes 1228824
  63.4 2.5 %own_terms.1 = (bf16[160,320]{1,0:T(8,128)(2,1)}, f32[160,320]{1,0:T(8,128)S(1)}, f32[160,320]{1,0:T(8,128)S(1)}) custom-call(bf16[160,320]{1,0:T(8,128)(2,1)S(1)} %gather_sum.1.grad_ref, bf16[480,320]{1,0:T(8,128)(2,1)S(1)} %copy-done.9, bf16[480,320]{1,0:T(8,128)(2,1)S(1)} %copy-done.6, bf16[480,320]{1,0:T(8,128)(2,1)S(1)} %copy-done.3, ...), custom_call_target="tpu_custom_call" | custom-call | tf_op jit(solution)/shard_map/own_terms/pallas_call | solution.py:330
  65.8 0.0 collective-permute-done.3.right_ref
  65.8 0.0 collective-permute-done.2.left_ref
  65.8 1.0 %copy-done.1 = bf16[2,960,80]{2,1,0:T(8,128)(2,1)S(1)} copy-done((bf16[2,960,80]{2,1,0:T(8,128)(2,1)S(1)}, bf16[2,960,80]{2,1,0:T(8,128)(2,1)}, u32[]{:S(2)}) %copy-start.1) | copy-done | bytes 307224
  66.9 1.0 %copy-done.4 = bf16[480,320]{1,0:T(8,128)(2,1)S(1)} copy-done((bf16[480,320]{1,0:T(8,128)(2,1)S(1)}, bf16[480,320]{1,0:T(8,128)(2,1)}, u32[]{:S(2)}) %copy-start.4) | copy-done | bytes 307224
  67.9 1.0 %copy-done.7 = bf16[480,320]{1,0:T(8,128)(2,1)S(1)} copy-done((bf16[480,320]{1,0:T(8,128)(2,1)S(1)}, bf16[480,320]{1,0:T(8,128)(2,1)}, u32[]{:S(2)}) %copy-start.7) | copy-done | bytes 307224
  68.8 1.2 %copy-done.11 = bf16[2,2,320,320]{3,2,1,0:T(8,128)(2,1)S(1)} copy-done((bf16[2,2,320,320]{3,2,1,0:T(8,128)(2,1)S(1)}, bf16[2,2,320,320]{3,2,1,0:T(8,128)(2,1)}, u32[]{:S(2)}) %copy-start.11) | copy-done | bytes 819224
  70.0 1.0 %copy-done.12 = f32[2,160,320]{2,1,0:T(8,128)S(1)} copy-done((f32[2,160,320]{2,1,0:T(8,128)S(1)}, f32[2,160,320]{2,1,0:T(8,128)}, u32[]{:S(2)}) %copy-start.12) | copy-done | bytes 409624
  71.1 2.1 %side_terms.1 = (bf16[160,320]{1,0:T(8,128)(2,1)}, bf16[160,320]{1,0:T(8,128)(2,1)}) custom-call(bf16[160,320]{1,0:T(8,128)(2,1)S(1)} %collective-permute-done.2.left_ref, bf16[160,320]{1,0:T(8,128)(2,1)S(1)} %collective-permute-done.3.right_ref, bf16[480,320]{1,0:T(8,128)(2,1)S(1)} %copy-done.7, bf16[480,320]{1,0:T(8,128)(2,1)S(1)} %copy-done.4, ...), custom_call_target="tpu_custom_call" | custom-call | tf_op jit(solution)/shard_map/side_terms/pallas_call | solution.py:365
  (23 shorter events, 0.1 us)
Async XLA Ops:
  0.6 16.3 %copy-start.15 = (bf16[320,160]{0,1:T(8,128)(2,1)S(1)}, bf16[320,160]{0,1:T(8,128)(2,1)}, u32[]{:S(2)}) copy-start(bf16[320,160]{0,1:T(8,128)(2,1)} %param.16) | copy-start | bytes 307204
  0.6 16.3 %copy-start.16 = (bf16[320,160]{0,1:T(8,128)(2,1)S(1)}, bf16[320,160]{0,1:T(8,128)(2,1)}, u32[]{:S(2)}) copy-start(bf16[320,160]{0,1:T(8,128)(2,1)} %param.15) | copy-start | bytes 307204
  0.7 16.3 %copy-start.17 = (bf16[320,160]{0,1:T(8,128)(2,1)S(1)}, bf16[320,160]{0,1:T(8,128)(2,1)}, u32[]{:S(2)}) copy-start(bf16[320,160]{0,1:T(8,128)(2,1)} %param.14) | copy-start | bytes 307204
  9.6 17.1 %all-to-all-start = ((bf16[8,24,640]{2,1,0:T(8,128)(2,1)}), bf16[8,24,640]{2,1,0:T(8,128)(2,1)S(1)}, u32[]{:S(2)}, u32[]{:S(2)}) async-start(bf16[8,24,640]{2,1,0:T(8,128)(2,1)} %down_product.1), calls=%async_computation | async-start | bytes 491520 | tf_op jit(solution)/shard_map/all_to_all | solution.py:396
  17.0 21.8 %copy-start.8 = (bf16[480,320]{1,0:T(8,128)(2,1)}, bf16[480,320]{1,0:T(8,128)(2,1)S(1)}, u32[]{:S(2)}) copy-start(bf16[480,320]{1,0:T(8,128)(2,1)S(1)} %pad_maximum_fusion.own_ref) | copy-start | bytes 921604
  17.0 21.7 %collective-permute-start.1 = (bf16[480,320]{1,0:T(8,128)(2,1)S(1)}, bf16[480,320]{1,0:T(8,128)(2,1)S(1)}, u32[]{:S(2)}, u32[]{:S(2)}) collective-permute-start(bf16[480,320]{1,0:T(8,128)(2,1)S(1)} %pad_maximum_fusion.own_ref), channel_id=1, source_target_pairs={{2,0},{4,2},{6,4},{3,1},{5,3},{7,5},{10,8},{12,10},{14,12},{11,9},... | collective-permute-start | bytes 921608 | tf_op jit(solution)/shard_map/ppermute | solution.py:380
  18.3 20.5 %collective-permute-start = (bf16[480,320]{1,0:T(8,128)(2,1)S(1)}, bf16[480,320]{1,0:T(8,128)(2,1)S(1)}, u32[]{:S(2)}, u32[]{:S(2)}) collective-permute-start(bf16[480,320]{1,0:T(8,128)(2,1)S(1)} %pad_maximum_fusion.own_ref), channel_id=1, source_target_pairs={{0,2},{2,4},{4,6},{1,3},{3,5},{5,7},{8,10},{10,12},{12,14},{9,11},... | collective-permute-start | bytes 921608 | tf_op jit(solution)/shard_map/ppermute | solution.py:379
  26.7 0.7 copy-start.14
  35.2 15.6 %all-to-all-start.1 = ((bf16[8,80,640]{2,1,0:T(8,128)(2,1)}), bf16[8,80,640]{2,1,0:T(8,128)(2,1)S(1)}, u32[]{:S(2)}, u32[]{:S(2)}) async-start(bf16[8,80,640]{2,1,0:T(8,128)(2,1)} %up_product.1), calls=%async_computation.1 | async-start | bytes 1638400 | tf_op jit(solution)/shard_map/all_to_all | solution.py:404
  38.7 0.8 %copy-start.2 = (bf16[480,320]{1,0:T(8,128)(2,1)}, bf16[480,320]{1,0:T(8,128)(2,1)S(1)}, u32[]{:S(2)}) copy-start(bf16[480,320]{1,0:T(8,128)(2,1)S(1)} %collective-permute-done.1.after_ref) | copy-start | bytes 921604
  38.8 0.9 %copy-start.5 = (bf16[480,320]{1,0:T(8,128)(2,1)}, bf16[480,320]{1,0:T(8,128)(2,1)S(1)}, u32[]{:S(2)}) copy-start(bf16[480,320]{1,0:T(8,128)(2,1)S(1)} %collective-permute-done.before_ref) | copy-start | bytes 921604
  50.8 0.7 copy-start.13
  51.9 13.9 %collective-permute-start.3 = (bf16[160,320]{1,0:T(8,128)(2,1)S(1)}, bf16[160,320]{1,0:T(8,128)(2,1)S(1)}, u32[]{:S(2)}, u32[]{:S(2)}) collective-permute-start(bf16[160,320]{1,0:T(8,128)(2,1)S(1)} %gather_sum.1.grad_ref), channel_id=1, source_target_pairs={{2,0},{4,2},{6,4},{3,1},{5,3},{7,5},{10,8},{12,10},{14,12},{11,9},... | collective-permute-start | bytes 307208 | tf_op jit(solution)/shard_map/ppermute | solution.py:380
  53.2 12.6 %collective-permute-start.2 = (bf16[160,320]{1,0:T(8,128)(2,1)S(1)}, bf16[160,320]{1,0:T(8,128)(2,1)S(1)}, u32[]{:S(2)}, u32[]{:S(2)}) collective-permute-start(bf16[160,320]{1,0:T(8,128)(2,1)S(1)} %gather_sum.1.grad_ref), channel_id=1, source_target_pairs={{0,2},{2,4},{4,6},{1,3},{3,5},{5,7},{8,10},{10,12},{12,14},{9,11},... | collective-permute-start | bytes 307208 | tf_op jit(solution)/shard_map/ppermute | solution.py:379
  58.0 1.0 %copy-start = (bf16[2,960,80]{2,1,0:T(8,128)(2,1)S(1)}, bf16[2,960,80]{2,1,0:T(8,128)(2,1)}, u32[]{:S(2)}) copy-start(bf16[2,960,80]{2,1,0:T(8,128)(2,1)} %get-tuple-element.23.values_ref) | copy-start | bytes 921604
  59.0 1.0 %copy-start.3 = (bf16[480,320]{1,0:T(8,128)(2,1)S(1)}, bf16[480,320]{1,0:T(8,128)(2,1)}, u32[]{:S(2)}) copy-start(bf16[480,320]{1,0:T(8,128)(2,1)} %copy-done.2) | copy-start | bytes 921604
  60.0 1.0 %copy-start.6 = (bf16[480,320]{1,0:T(8,128)(2,1)S(1)}, bf16[480,320]{1,0:T(8,128)(2,1)}, u32[]{:S(2)}) copy-start(bf16[480,320]{1,0:T(8,128)(2,1)} %copy-done.5) | copy-start | bytes 921604
  61.0 1.0 %copy-start.9 = (bf16[480,320]{1,0:T(8,128)(2,1)S(1)}, bf16[480,320]{1,0:T(8,128)(2,1)}, u32[]{:S(2)}) copy-start(bf16[480,320]{1,0:T(8,128)(2,1)} %copy-done.8) | copy-start | bytes 921604
  62.0 1.4 %copy-start.10 = (bf16[2,960,320]{2,1,0:T(8,128)(2,1)S(1)}, bf16[2,960,320]{2,1,0:T(8,128)(2,1)}, u32[]{:S(2)}) copy-start(bf16[2,960,320]{2,1,0:T(8,128)(2,1)} %get-tuple-element.22.probs_ref) | copy-start | bytes 3686404
  65.8 1.0 %copy-start.1 = (bf16[2,960,80]{2,1,0:T(8,128)(2,1)S(1)}, bf16[2,960,80]{2,1,0:T(8,128)(2,1)}, u32[]{:S(2)}) copy-start(bf16[2,960,80]{2,1,0:T(8,128)(2,1)} %get-tuple-element.23.values_ref) | copy-start | bytes 921604
  66.9 1.0 %copy-start.4 = (bf16[480,320]{1,0:T(8,128)(2,1)S(1)}, bf16[480,320]{1,0:T(8,128)(2,1)}, u32[]{:S(2)}) copy-start(bf16[480,320]{1,0:T(8,128)(2,1)} %copy-done.2) | copy-start | bytes 921604
  67.9 1.0 %copy-start.7 = (bf16[480,320]{1,0:T(8,128)(2,1)S(1)}, bf16[480,320]{1,0:T(8,128)(2,1)}, u32[]{:S(2)}) copy-start(bf16[480,320]{1,0:T(8,128)(2,1)} %copy-done.5) | copy-start | bytes 921604
  68.8 1.2 %copy-start.11 = (bf16[2,2,320,320]{3,2,1,0:T(8,128)(2,1)S(1)}, bf16[2,2,320,320]{3,2,1,0:T(8,128)(2,1)}, u32[]{:S(2)}) copy-start(bf16[2,2,320,320]{3,2,1,0:T(8,128)(2,1)} %get-tuple-element.25.probs_ref) | copy-start | bytes 2457604
  70.0 1.0 %copy-start.12 = (f32[2,160,320]{2,1,0:T(8,128)S(1)}, f32[2,160,320]{2,1,0:T(8,128)}, u32[]{:S(2)}) copy-start(f32[2,160,320]{2,1,0:T(8,128)} %get-tuple-element.26.attended_ref) | copy-start | bytes 1228804

commit v3 on v2

--- a/solution.py
+++ b/solution.py
@@ -47,9 +47,6 @@
     offsets = min(groups, row_count // 2)
     capacity = row_count // offsets
     return capacity, -(-(capacity + 1) // 8) * 8
-
-
-DONE = jax.ShapeDtypeStruct((8, 128), jnp.float32)
 
 
 def one_product(count, slots, hidden):
@@ -175,7 +172,7 @@
             pltpu.VMEM((heads, width, weight.shape[1]), jnp.bfloat16),
             pltpu.SemaphoreType.DMA((heads * 4,)),
         ],
-        compiler_params=params(60),
+        compiler_params=params(52),
         cost_estimate=pl.CostEstimate(
             flops=8 * pre.shape[0] * weight.size, bytes_accessed=8 * weight.size, transcendentals=0
         ),
@@ -183,10 +180,37 @@
     )(pieces, pre, weight)
 
 
-def softmax_kernel(lengths_ref, first_ref, own_ref, before_ref, after_ref, own_probs_out,
-                   side_probs_out, attended_out, values_out, done_ref, own_probs_ref,
-                   side_probs_ref, attended_ref, values_ref, sems):
-    columns, patches = own_ref.shape[0] // 3, own_ref.shape[1]
+class Rows:
+    def __init__(self, columns, patches):
+        heads = columns // HEAD_DIM
+        self.columns, self.patches = columns, patches
+        self.probs_at = 9 * columns
+        self.side_at = self.probs_at + heads * 3 * patches
+        self.attended_at = self.side_at + heads * 2 * patches
+        self.total = self.attended_at + 2 * columns
+
+    def block(self, b, kind):
+        return pl.ds((3 * b + kind) * self.columns, self.columns)
+
+    def blocks(self, b):
+        return pl.ds(3 * b * self.columns, 3 * self.columns)
+
+    def probs(self, h):
+        return pl.ds(self.probs_at + h * 3 * self.patches, 3 * self.patches)
+
+    def side_probs(self, h):
+        return pl.ds(self.side_at + h * 2 * self.patches, 2 * self.patches)
+
+    def attended(self):
+        return pl.ds(self.attended_at, 2 * self.columns)
+
+
+def softmax_kernel(lengths_ref, first_ref, own_hbm, before_hbm, after_hbm, out_hbm, held, sems):
+    columns, patches = own_hbm.shape[0] // 3, own_hbm.shape[1]
+    heads = columns // HEAD_DIM
+    rows = Rows(columns, patches)
+    pairs = [(x, held.at[rows.blocks(b)]) for b, x in enumerate((own_hbm, before_hbm, after_hbm))]
+    copies = fetched(pairs, sems)
     first = first_ref[0, 0]
 
     def image_of(shape, dim):
@@ -202,74 +226,63 @@
 
     key_image = image_of((3 * patches, 1), 0)
     query_image = image_of((1, 3 * patches), 1)
-    blocks = (before_ref, own_ref, after_ref)
-    heads = columns // HEAD_DIM
+    for copy in copies:
+        copy.wait()
+    at = (1, 0, 2)
     for h in range(heads):
-        q, k, v = [
-            [b[t * columns + h * HEAD_DIM : t * columns + (h + 1) * HEAD_DIM] for b in blocks]
-            for t in range(3)
-        ]
-        rows_of = lambda x: x.astype(jnp.float32).T.astype(jnp.bfloat16)
-        k_rows = [rows_of(x) for x in k]
-        for b in range(3):
-            values_ref[h, b * patches : (b + 1) * patches] = rows_of(v[b])
-        for qb, keys in ((0, (0, 1)), (1, (0, 1, 2)), (2, (1, 2))):
+
+        def part(b, kind):
+            start = (3 * b + kind) * columns + h * HEAD_DIM
+            return held[start : start + HEAD_DIM]
+
+        k_rows = [part(b, 1).astype(jnp.float32).T.astype(jnp.bfloat16) for b in range(3)]
+        for qb, keys in ((1, (1, 0)), (0, (1, 0, 2)), (2, (0, 2))):
             scores = []
-            image = query_image[:, qb * patches : (qb + 1) * patches]
+            image = query_image[:, at[qb] * patches : (at[qb] + 1) * patches]
             for kb in keys:
-                same = key_image[kb * patches : (kb + 1) * patches] == image
-                scores.append(jnp.where(same, dot(k_rows[kb], q[qb], NN) * SCALE, -jnp.inf))
+                same = key_image[at[kb] * patches : (at[kb] + 1) * patches] == image
+                products = dot(k_rows[kb], part(qb, 0), NN) * SCALE
+                scores.append(jnp.where(same, products, -jnp.inf))
             tops = [jnp.max(s, 0, keepdims=True) for s in scores]
             top = functools.reduce(jnp.maximum, tops)
             weights = [jnp.exp(s - top) for s in scores]
             over = 1.0 / functools.reduce(jnp.add, [jnp.sum(w, 0, keepdims=True) for w in weights])
             attended = jnp.zeros((HEAD_DIM, patches), jnp.float32)
-            for kb, w in zip(keys, weights):
+            for n, (kb, w) in enumerate(zip(keys, weights)):
                 probs = (w * over).astype(jnp.bfloat16)
-                if qb == 1:
-                    own_probs_ref[h, kb * patches : (kb + 1) * patches] = probs
+                if qb == 0:
+                    start = rows.probs_at + (3 * h + n) * patches
+                    held[start : start + patches] = probs
                 else:
-                    attended = attended + dot(v[kb], probs, NN)
-                    if kb == 1:
-                        side_probs_ref[h, qb // 2] = probs
-            if qb != 1:
-                attended_ref[qb // 2, h * HEAD_DIM : (h + 1) * HEAD_DIM] = attended
-    pairs = (
-        (own_probs_ref, own_probs_out),
-        (side_probs_ref, side_probs_out),
-        (attended_ref, attended_out),
-        (values_ref, values_out),
-    )
-    copies = [pltpu.make_async_copy(a, b, sems.at[i]) for i, (a, b) in enumerate(pairs)]
-    for copy in copies:
-        copy.start()
-    for copy in copies:
-        copy.wait()
-    done_ref[...] = jnp.zeros(done_ref.shape, jnp.float32)
+                    attended = attended + dot(part(kb, 2), probs, NN)
+                    if kb == 0:
+                        start = rows.side_at + (2 * h + qb - 1) * patches
+                        held[start : start + patches] = probs
+            if qb != 0:
+                start = rows.attended_at + (qb - 1) * columns + h * HEAD_DIM
+                held[start : start + HEAD_DIM] = attended.astype(jnp.bfloat16)
+    out = pltpu.make_async_copy(held, out_hbm, sems.at[3])
+    out.start()
+    out.wait()
 
 
 def softmax_parts(lengths, first, own, before, after):
     columns, patches = own.shape[0] // 3, own.shape[1]
-    heads = columns // HEAD_DIM
+    rows = Rows(columns, patches)
     smem = pl.BlockSpec(memory_space=pltpu.MemorySpace.SMEM)
-    shapes = (
-        jax.ShapeDtypeStruct((heads, 3 * patches, patches), jnp.bfloat16),
-        jax.ShapeDtypeStruct((heads, 2, patches, patches), jnp.bfloat16),
-        jax.ShapeDtypeStruct((2, columns, patches), jnp.float32),
-        jax.ShapeDtypeStruct((heads, 3 * patches, HEAD_DIM), jnp.bfloat16),
-    )
+    work = (columns // HEAD_DIM) * patches * patches
     return pl.pallas_call(
         softmax_kernel,
-        out_shape=shapes + (DONE,),
-        in_specs=[smem, smem] + in_vmem(3),
-        out_specs=tuple(in_hbm(4) + in_vmem(1)),
-        scratch_shapes=[pltpu.VMEM(x.shape, x.dtype) for x in shapes]
-        + [pltpu.SemaphoreType.DMA((4,))],
+        out_shape=jax.ShapeDtypeStruct((rows.total, patches), jnp.bfloat16),
+        in_specs=[smem, smem] + in_hbm(3),
+        out_specs=in_hbm(1)[0],
+        scratch_shapes=[
+            pltpu.VMEM((rows.total, patches), jnp.bfloat16),
+            pltpu.SemaphoreType.DMA((4,)),
+        ],
         compiler_params=params(60),
         cost_estimate=pl.CostEstimate(
-            flops=100_000 * heads * patches * patches,
-            bytes_accessed=500 * heads * patches * patches,
-            transcendentals=9 * heads * patches * patches,
+            flops=100_000 * work, bytes_accessed=500 * work, transcendentals=9 * work
         ),
         name="softmax_parts",
     )(lengths.reshape(1, -1), first.reshape(1, 1), own, before, after)
@@ -296,37 +309,49 @@
     return pl.pallas_call(
         gather_kernel,
         out_shape=jax.ShapeDtypeStruct((width // 4, 4 * row_count), jnp.bfloat16),
-        in_specs=in_vmem(2),
+        in_specs=in_vmem(1) + in_hbm(1),
         out_specs=pl.BlockSpec(memory_space=VMEM),
-        compiler_params=params(16),
+        compiler_params=params(52),
         name="gather_sum",
     )(pieces, later)
 
 
-def own_kernel(grad_ref, own_ref, before_ref, after_ref, probs_ref, values_ref,
-               query_ref, key_ref, value_ref):
+def own_kernel(grad_ref, held_hbm, query_ref, key_ref, value_ref, probs_ref, blocks_ref, own_ref,
+               sems):
     columns, patches = grad_ref.shape
-    blocks = (before_ref, own_ref, after_ref)
-    for h in range(columns // HEAD_DIM):
+    heads = columns // HEAD_DIM
+    rows = Rows(columns, patches)
+    pairs = [(held_hbm.at[rows.block(b, 2)], blocks_ref.at[1, i]) for i, b in enumerate((1, 0, 2))]
+    pairs += [(held_hbm.at[rows.probs(h)], probs_ref.at[h]) for h in range(heads)]
+    pairs += [(held_hbm.at[rows.block(b, 1)], blocks_ref.at[0, i]) for i, b in enumerate((1, 0, 2))]
+    pairs += [(held_hbm.at[rows.block(0, 0)], own_ref)]
+    copies = fetched(pairs, sems)
+    for copy in copies[:3]:
+        copy.wait()
+    for h in range(heads):
         cols = slice(h * HEAD_DIM, (h + 1) * HEAD_DIM)
         grad = grad_ref[cols]
-        rows = [slice(b * patches, (b + 1) * patches) for b in range(3)]
-        slopes = [dot(values_ref[h, r], grad, NN) for r in rows]
-        probs = [probs_ref[h, r] for r in rows]
+        slopes = [dot(blocks_ref[1, b, cols], grad, TN) for b in range(3)]
+        copies[3 + h].wait()
+        probs = [probs_ref[h, b * patches : (b + 1) * patches] for b in range(3)]
         wide = [p.astype(jnp.float32) for p in probs]
         delta = sum([jnp.sum(p * s, 0, keepdims=True) for p, s in zip(wide, slopes)])
+        if h == 0:
+            for copy in copies[3 + heads :]:
+                copy.wait()
         total = jnp.zeros((HEAD_DIM, patches), jnp.float32)
-        for b, ref in enumerate(blocks):
+        for b in range(3):
             scores = (wide[b] * (slopes[b] - delta)).astype(jnp.bfloat16)
-            key = ref[columns + h * HEAD_DIM : columns + (h + 1) * HEAD_DIM]
-            total = total + dot(key, scores, NN)
+            total = total + dot(blocks_ref[0, b, cols], scores, NN)
             if b == 1:
-                key_ref[cols] = dot(ref[cols], scores, NT)
+                key_ref[cols] = dot(own_ref[cols], scores, NT)
                 value_ref[cols] = dot(grad, probs[b], NT)
         query_ref[cols] = (total * SCALE).astype(jnp.bfloat16)
 
 
-def own_terms(grad, own, before, after, probs, values):
+def own_terms(grad, held):
+    heads = grad.shape[0] // HEAD_DIM
+    columns, patches = grad.shape
     return pl.pallas_call(
         own_kernel,
         out_shape=(
@@ -334,42 +359,73 @@
             jax.ShapeDtypeStruct(grad.shape, jnp.float32),
             jax.ShapeDtypeStruct(grad.shape, jnp.float32),
         ),
-        in_specs=in_vmem(6),
+        in_specs=in_vmem(1) + in_hbm(1),
         out_specs=tuple(in_vmem(3)),
-        compiler_params=params(32),
+        scratch_shapes=[
+            pltpu.VMEM((heads, 3 * patches, patches), jnp.bfloat16),
+            pltpu.VMEM((2, 3, columns, patches), jnp.bfloat16),
+            pltpu.VMEM(grad.shape, jnp.bfloat16),
+            pltpu.SemaphoreType.DMA((7 + heads,)),
+        ],
+        compiler_params=params(52),
         name="own_terms",
-    )(grad, own, before, after, probs, values)
-
-
-def side_kernel(left_ref, right_ref, before_ref, after_ref, probs_ref, attended_ref, values_ref,
-                key_part_ref, value_part_ref, key_ref, value_ref):
+    )(grad, held)
+
+
+def side_kernel(left_ref, right_ref, key_part_ref, value_part_ref, held_hbm, key_ref, value_ref,
+                values_ref, attended_ref, probs_ref, queries_ref, sems):
     columns, patches = left_ref.shape
-    for h in range(columns // HEAD_DIM):
+    heads = columns // HEAD_DIM
+    rows = Rows(columns, patches)
+    pairs = [(held_hbm.at[rows.block(0, 2)], values_ref), (held_hbm.at[rows.attended()], attended_ref)]
+    pairs += [(held_hbm.at[rows.side_probs(h)], probs_ref.at[h]) for h in range(heads)]
+    pairs += [(held_hbm.at[rows.block(1 + i, 0)], queries_ref.at[i]) for i in range(2)]
+    copies = fetched(pairs, sems)
+    copies[0].wait()
+    for h in range(heads):
         cols = slice(h * HEAD_DIM, (h + 1) * HEAD_DIM)
+        grads = (left_ref[cols], right_ref[cols])
+        slopes = [dot(values_ref[cols], grad, TN) for grad in grads]
         key, value = key_part_ref[cols], value_part_ref[cols]
-        for side, (grad_ref, ref) in enumerate(((left_ref, before_ref), (right_ref, after_ref))):
-            grad = grad_ref[cols]
-            attended = attended_ref[side, cols]
+        if h == 0:
+            copies[1].wait()
+        copies[2 + h].wait()
+        scores = []
+        for side, grad in enumerate(grads):
+            start = side * columns + h * HEAD_DIM
+            attended = attended_ref[start : start + HEAD_DIM].astype(jnp.float32)
             delta = jnp.sum(grad.astype(jnp.float32) * attended, 0, keepdims=True)
-            probs = probs_ref[h, side]
-            slope = dot(values_ref[h, patches : 2 * patches], grad, NN)
-            scores = (probs.astype(jnp.float32) * (slope - delta)).astype(jnp.bfloat16)
-            key = key + dot(ref[cols], scores, NT)
+            probs = probs_ref[h, side * patches : (side + 1) * patches]
+            scores.append((probs.astype(jnp.float32) * (slopes[side] - delta)).astype(jnp.bfloat16))
             value = value + dot(grad, probs, NT)
+        if h == 0:
+            for copy in copies[2 + heads :]:
+                copy.wait()
+        for side in range(2):
+            key = key + dot(queries_ref[side, cols], scores[side], NT)
         key_ref[cols] = (key * SCALE).astype(jnp.bfloat16)
         value_ref[cols] = value.astype(jnp.bfloat16)
 
 
-def side_terms(left, right, before, after, probs, attended, values, key_part, value_part):
+def side_terms(left, right, key_part, value_part, held):
     shape = jax.ShapeDtypeStruct(left.shape, jnp.bfloat16)
+    columns, patches = left.shape
+    heads = columns // HEAD_DIM
     return pl.pallas_call(
         side_kernel,
         out_shape=(shape, shape),
-        in_specs=in_vmem(9),
+        in_specs=in_vmem(4) + in_hbm(1),
         out_specs=tuple(in_vmem(2)),
-        compiler_params=params(32),
+        scratch_shapes=[
+            pltpu.VMEM(left.shape, jnp.bfloat16),
+            pltpu.VMEM((2 * columns, patches), jnp.bfloat16),
+            pltpu.VMEM((heads, 2 * patches, patches), jnp.bfloat16),
+            pltpu.VMEM((2,) + left.shape, jnp.bfloat16),
+            pltpu.SemaphoreType.DMA((4 + heads,)),
+        ],
+        compiler_params=params(52),
         name="side_terms",
-    )(left, right, before, after, probs, attended, values, key_part, value_part)
+    )(left, right, key_part, value_part, held)
 
 
 def from_both_sides(x, axis):
@@ -397,17 +453,13 @@
     own = jnp.concatenate([queries.T, key_states.T, value_states.T], 0)
     before, after = from_both_sides(own, "grp")
     first = (lax.axis_index("grp") - 1) * row_count
-    own_probs, side_probs, attended, values, softmax_done = softmax_parts(
-        lengths, first, own, before, after
-    )
+    held = softmax_parts(lengths, first, own, before, after)
     shares = up_pieces(arrived, pre_act, w_up, heads, capacity)
     shares = lax.all_to_all(shares, ("sect", "span"), split_axis=0, concat_axis=0, tiled=True)
-    grad = gathered(shares, softmax_done)
+    grad = gathered(shares, held)
     left, right = from_both_sides(grad, "grp")
-    grad_query, key_part, value_part = own_terms(grad, own, before, after, own_probs, values)
-    grad_key, grad_value = side_terms(
-        left, right, before, after, side_probs, attended, values, key_part, value_part
-    )
+    grad_query, key_part, value_part = own_terms(grad, held)
+    grad_key, grad_value = side_terms(left, right, key_part, value_part, held)
     return grad_query.T, grad_key.T, grad_value.T
 
 

time: 74 us -> 61.9 us (0.84)
  local copies, waits for them, and re-layouts: 12.8 us -> 0.88 us
  starting transfers between devices: 22.7 us -> 20.4 us
  waiting for transfers between devices: 5.63 us -> 7.83 us
    unnamed x36 -> x14, local copies, waits for them, and re-layouts: 12.8 us -> 0.88 us
    ppermute x2, starting transfers between devices: 9.3 us -> 6.75 us  [from_both_sides(): lax.ppermute(x, axis, up)]
    ppermute x2, waiting for transfers between devices: 0.01 us -> 1.58 us  [from_both_sides(): lax.ppermute(x, axis, [(j, i) for i, j in up])]
    pallas_call x1, Pallas kernels: 2.47 us -> 3.77 us  [own_terms(): pl.pallas_call(own_kernel, out_shape=(jax.ShapeDtypeStruct(grad.shape, jn...]
    all_to_all x1, waiting for transfers between devices: 1.77 us -> 2.88 us  [on_device(): lax.all_to_all(shares, ('sect', 'span'), split_axis=0, concat_axis=0, til...]
    pallas_call x1, Pallas kernels: 7.72 us -> 6.73 us  [up_pieces(): pl.pallas_call(functools.partial(up_kernel, heads, capacity), out_shape=j...]
  transfers between devices with their start and end apart: 6 -> 6, of which waited for: 2 -> 3; matrix products, arithmetic and copies ran while one was open for 0% -> 0% of each run, Pallas kernels for 27% -> 31%
where the time goes in v3:
time: 61.9 us; the launch traced here: 61.5 us
  Pallas kernels  31.4 us (51%)
  starting transfers between devices  20.4 us (33%)
  waiting for transfers between devices  7.83 us (13%)
  between operations  0.99 us (2%)
  local copies, waits for them, and re-layouts  0.88 us (1%)
    pallas_call x1, Pallas kernels, down_pieces(): pl.pallas_call(functools.partial(down_kernel, groups, spans, capacity, sl...  8.95 us
    pallas_call x1, Pallas kernels, softmax_parts(): pl.pallas_call(softmax_kernel, out_shape=jax.ShapeDtypeStruct((rows.total...  8.27 us
    all_to_all x1, starting transfers between devices, on_device(): lax.all_to_all(pieces, ('grp', 'span'), split_axis=0, concat_axis=0, tile...  7.3 us
    ppermute x2, starting transfers between devices, from_both_sides(): lax.ppermute(x, axis, up)  6.75 us
    pallas_call x1, Pallas kernels, up_pieces(): pl.pallas_call(functools.partial(up_kernel, heads, capacity), out_shape=j...  6.73 us
    pallas_call x1, Pallas kernels, own_terms(): pl.pallas_call(own_kernel, out_shape=(jax.ShapeDtypeStruct(grad.shape, jn...  3.77 us
    all_to_all x1, starting transfers between devices, on_device(): lax.all_to_all(shares, ('sect', 'span'), split_axis=0, concat_axis=0, til...  3.56 us
    all_to_all x1, waiting for transfers between devices, on_device(): lax.all_to_all(pieces, ('grp', 'span'), split_axis=0, concat_axis=0, tile...  3.36 us
  transfers between devices with their start and end apart: 6, of which 3 were waited for; matrix products, arithmetic and copies ran while one was open for 0% of the time, Pallas kernels for 31%

profile of v3, /device:TPU:0, one launch (start us, length us, event | category | flops | bytes accessed | tf_op | source)
XLA Modules:
  0.0 61.5 jit_solution(58443817504785404)
XLA Ops:
  0.6 0.0 copy-start.4
  0.6 0.0 copy-start.3
  0.7 0.0 copy-start.2
  0.7 0.0 copy-start
  0.7 9.0 %down_product.1 = bf16[8,24,640]{2,1,0:T(8,128)(2,1)} custom-call(s32[1,80]{1,0:T(1,128)} %bitcast.12, bf16[80,4096]{1,0:T(8,128)(2,1)} %rows_hbm.1, bf16[1280,4096]{1,0:T(8,128)(2,1)} %weight_ref.2), custom_call_target="tpu_custom_call" | custom-call | tf_op jit(solution)/shard_map/down_product/pallas_call | solution.py:107
  9.6 7.3 %all-to-all-start = ((bf16[8,24,640]{2,1,0:T(8,128)(2,1)}), bf16[8,24,640]{2,1,0:T(8,128)(2,1)S(1)}, u32[]{:S(2)}, u32[]{:S(2)}) async-start(bf16[8,24,640]{2,1,0:T(8,128)(2,1)} %down_product.1), calls=%async_computation | async-start | bytes 491520 | tf_op jit(solution)/shard_map/all_to_all | solution.py:452
  16.9 0.0 copy-done.4
  16.9 0.0 copy-done.3
  16.9 0.0 copy-done.2
  17.0 0.0 copy-start.1
  17.0 3.9 %collective-permute-start = (bf16[480,320]{1,0:T(8,128)(2,1)S(1)}, bf16[480,320]{1,0:T(8,128)(2,1)S(1)}, u32[]{:S(2)}, u32[]{:S(2)}) collective-permute-start(bf16[480,320]{1,0:T(8,128)(2,1)S(1)} %pad_maximum_fusion.own_hbm), channel_id=1, source_target_pairs={{0,2},{2,4},{4,6},{1,3},{3,5},{5,7},{8,10},{10,12},{12,14},{9,11},... | collective-permute-start | bytes 921608 | tf_op jit(solution)/shard_map/ppermute | solution.py:435
  21.0 1.3 %collective-permute-start.1 = (bf16[480,320]{1,0:T(8,128)(2,1)S(1)}, bf16[480,320]{1,0:T(8,128)(2,1)S(1)}, u32[]{:S(2)}, u32[]{:S(2)}) collective-permute-start(bf16[480,320]{1,0:T(8,128)(2,1)S(1)} %pad_maximum_fusion.own_hbm), channel_id=1, source_target_pairs={{2,0},{4,2},{6,4},{3,1},{5,3},{7,5},{10,8},{12,10},{14,12},{11,9},... | collective-permute-start | bytes 921608 | tf_op jit(solution)/shard_map/ppermute | solution.py:436
  22.3 3.4 %all-to-all-done.pieces_ref = bf16[8,24,640]{2,1,0:T(8,128)(2,1)S(1)} async-done(((bf16[8,24,640]{2,1,0:T(8,128)(2,1)}), bf16[8,24,640]{2,1,0:T(8,128)(2,1)S(1)}, u32[]{:S(2)}, u32[]{:S(2)}) %all-to-all-start) | async-done | bytes 245792 | tf_op jit(solution)/shard_map/all_to_all | solution.py:452
  25.6 0.0 copy-done
  25.6 6.7 %up_product.1 = bf16[8,80,640]{2,1,0:T(8,128)(2,1)} custom-call(bf16[8,24,640]{2,1,0:T(8,128)(2,1)S(1)} %all-to-all-done.pieces_ref, bf16[80,640]{1,0:T(8,128)(2,1)S(1)} %copy-done, bf16[5120,640]{1,0:T(8,128)(2,1)} %weight_ref.3), custom_call_target="tpu_custom_call" | custom-call | flops 2097152000 | bytes 26214400 | tf_op jit(solution)/shard_map/up_product/pallas_call | solution.py:166
  32.4 3.6 %all-to-all-start.1 = ((bf16[8,80,640]{2,1,0:T(8,128)(2,1)}), bf16[8,80,640]{2,1,0:T(8,128)(2,1)S(1)}, u32[]{:S(2)}, u32[]{:S(2)}) async-start(bf16[8,80,640]{2,1,0:T(8,128)(2,1)} %up_product.1), calls=%async_computation.1 | async-start | bytes 1638400 | tf_op jit(solution)/shard_map/all_to_all | solution.py:458
  35.9 0.0 collective-permute-done.before_hbm
  36.0 0.0 copy-start.5
  36.0 0.0 collective-permute-done.1.after_hbm
  36.0 0.0 copy-start.6
  36.0 0.0 copy-done.1
  36.0 0.7 %copy-done.5 = bf16[480,320]{1,0:T(8,128)(2,1)} copy-done((bf16[480,320]{1,0:T(8,128)(2,1)}, bf16[480,320]{1,0:T(8,128)(2,1)S(1)}, u32[]{:S(2)}) %copy-start.5) | copy-done | bytes 307224
  36.7 0.1 copy-done.6
  36.9 8.3 %softmax_parts.1._.held_hbm = bf16[4960,320]{1,0:T(8,128)(2,1)} custom-call(s32[1,12]{1,0:T(1,128)} %bitcast.16, s32[1,1]{1,0:T(1,128)} %bitcast.2.first_ref, bf16[480,320]{1,0:T(8,128)(2,1)} %copy-done.1, bf16[480,320]{1,0:T(8,128)(2,1)} %copy-done.5, bf16[480,320]{1,0:T(8,128)(2,1)} %copy-done.6), custom_call_target="tpu_custom_call" | custom-call | flops 20480000000 | bytes 102400000 | tf_op jit(solution)/shard_map/softmax_parts/pallas_call | solution.py:274
  45.1 2.9 %all-to-all-done.1.pieces_ref = bf16[8,80,640]{2,1,0:T(8,128)(2,1)S(1)} async-done(((bf16[8,80,640]{2,1,0:T(8,128)(2,1)}), bf16[8,80,640]{2,1,0:T(8,128)(2,1)S(1)}, u32[]{:S(2)}, u32[]{:S(2)}) %all-to-all-start.1) | async-done | bytes 819232 | tf_op jit(solution)/shard_map/all_to_all | solution.py:458
  48.0 0.5 gather_sum.1.grad_ref
  48.5 2.8 %collective-permute-start.2 = (bf16[160,320]{1,0:T(8,128)(2,1)S(1)}, bf16[160,320]{1,0:T(8,128)(2,1)S(1)}, u32[]{:S(2)}, u32[]{:S(2)}) collective-permute-start(bf16[160,320]{1,0:T(8,128)(2,1)S(1)} %gather_sum.1.grad_ref), channel_id=1, source_target_pairs={{0,2},{2,4},{4,6},{1,3},{3,5},{5,7},{8,10},{10,12},{12,14},{9,11},... | collective-permute-start | bytes 307208 | tf_op jit(solution)/shard_map/ppermute | solution.py:435
  51.3 1.5 %collective-permute-start.3 = (bf16[160,320]{1,0:T(8,128)(2,1)S(1)}, bf16[160,320]{1,0:T(8,128)(2,1)S(1)}, u32[]{:S(2)}, u32[]{:S(2)}) collective-permute-start(bf16[160,320]{1,0:T(8,128)(2,1)S(1)} %gather_sum.1.grad_ref), channel_id=1, source_target_pairs={{2,0},{4,2},{6,4},{3,1},{5,3},{7,5},{10,8},{12,10},{14,12},{11,9},... | collective-permute-start | bytes 307208 | tf_op jit(solution)/shard_map/ppermute | solution.py:436
  52.8 3.8 %own_terms.1 = (bf16[160,320]{1,0:T(8,128)(2,1)}, f32[160,320]{1,0:T(8,128)S(1)}, f32[160,320]{1,0:T(8,128)S(1)}) custom-call(bf16[160,320]{1,0:T(8,128)(2,1)S(1)} %gather_sum.1.grad_ref, bf16[4960,320]{1,0:T(8,128)(2,1)} %softmax_parts.1._.held_hbm), custom_call_target="tpu_custom_call" | custom-call | tf_op jit(solution)/shard_map/own_terms/pallas_call | solution.py:355
  56.6 0.0 collective-permute-done.2.left_ref
  56.6 1.6 %collective-permute-done.3.right_ref = bf16[160,320]{1,0:T(8,128)(2,1)S(1)} collective-permute-done((bf16[160,320]{1,0:T(8,128)(2,1)S(1)}, bf16[160,320]{1,0:T(8,128)(2,1)S(1)}, u32[]{:S(2)}, u32[]{:S(2)}) %collective-permute-start.3) | collective-permute-done | bytes 102432 | tf_op jit(solution)/shard_map/ppermute | solution.py:436
  58.2 3.2 %side_terms.1 = (bf16[160,320]{1,0:T(8,128)(2,1)}, bf16[160,320]{1,0:T(8,128)(2,1)}) custom-call(bf16[160,320]{1,0:T(8,128)(2,1)S(1)} %collective-permute-done.2.left_ref, bf16[160,320]{1,0:T(8,128)(2,1)S(1)} %collective-permute-done.3.right_ref, f32[160,320]{1,0:T(8,128)S(1)} %get-tuple-element.17.key_part_ref, ...), custom_call_target="tpu_custom_call" | custom-call | tf_op jit(solution)/shard_map/side_terms/pallas_call | solution.py:414
  (1 shorter events, 0.0 us)
Async XLA Ops:
  0.6 16.3 %copy-start.4 = (bf16[320,160]{0,1:T(8,128)(2,1)S(1)}, bf16[320,160]{0,1:T(8,128)(2,1)}, u32[]{:S(2)}) copy-start(bf16[320,160]{0,1:T(8,128)(2,1)} %param.14) | copy-start | bytes 307204
  0.6 16.3 %copy-start.3 = (bf16[320,160]{0,1:T(8,128)(2,1)S(1)}, bf16[320,160]{0,1:T(8,128)(2,1)}, u32[]{:S(2)}) copy-start(bf16[320,160]{0,1:T(8,128)(2,1)} %param.15) | copy-start | bytes 307204
  0.7 16.3 %copy-start.2 = (bf16[320,160]{0,1:T(8,128)(2,1)S(1)}, bf16[320,160]{0,1:T(8,128)(2,1)}, u32[]{:S(2)}) copy-start(bf16[320,160]{0,1:T(8,128)(2,1)} %param.16) | copy-start | bytes 307204
  0.7 25.0 %copy-start = (bf16[80,640]{1,0:T(8,128)(2,1)S(1)}, bf16[80,640]{1,0:T(8,128)(2,1)}, u32[]{:S(2)}) copy-start(bf16[80,640]{1,0:T(8,128)(2,1)} %pre_ref.1) | copy-start | bytes 307204
  9.6 16.0 %all-to-all-start = ((bf16[8,24,640]{2,1,0:T(8,128)(2,1)}), bf16[8,24,640]{2,1,0:T(8,128)(2,1)S(1)}, u32[]{:S(2)}, u32[]{:S(2)}) async-start(bf16[8,24,640]{2,1,0:T(8,128)(2,1)} %down_product.1), calls=%async_computation | async-start | bytes 491520 | tf_op jit(solution)/shard_map/all_to_all | solution.py:452
  17.0 19.0 %copy-start.1 = (bf16[480,320]{1,0:T(8,128)(2,1)}, bf16[480,320]{1,0:T(8,128)(2,1)S(1)}, u32[]{:S(2)}) copy-start(bf16[480,320]{1,0:T(8,128)(2,1)S(1)} %pad_maximum_fusion.own_hbm) | copy-start | bytes 921604
  17.0 18.9 %collective-permute-start = (bf16[480,320]{1,0:T(8,128)(2,1)S(1)}, bf16[480,320]{1,0:T(8,128)(2,1)S(1)}, u32[]{:S(2)}, u32[]{:S(2)}) collective-permute-start(bf16[480,320]{1,0:T(8,128)(2,1)S(1)} %pad_maximum_fusion.own_hbm), channel_id=1, source_target_pairs={{0,2},{2,4},{4,6},{1,3},{3,5},{5,7},{8,10},{10,12},{12,14},{9,11},... | collective-permute-start | bytes 921608 | tf_op jit(solution)/shard_map/ppermute | solution.py:435
  21.0 15.0 %collective-permute-start.1 = (bf16[480,320]{1,0:T(8,128)(2,1)S(1)}, bf16[480,320]{1,0:T(8,128)(2,1)S(1)}, u32[]{:S(2)}, u32[]{:S(2)}) collective-permute-start(bf16[480,320]{1,0:T(8,128)(2,1)S(1)} %pad_maximum_fusion.own_hbm), channel_id=1, source_target_pairs={{2,0},{4,2},{6,4},{3,1},{5,3},{7,5},{10,8},{12,10},{14,12},{11,9},... | collective-permute-start | bytes 921608 | tf_op jit(solution)/shard_map/ppermute | solution.py:436
  32.4 15.6 %all-to-all-start.1 = ((bf16[8,80,640]{2,1,0:T(8,128)(2,1)}), bf16[8,80,640]{2,1,0:T(8,128)(2,1)S(1)}, u32[]{:S(2)}, u32[]{:S(2)}) async-start(bf16[8,80,640]{2,1,0:T(8,128)(2,1)} %up_product.1), calls=%async_computation.1 | async-start | bytes 1638400 | tf_op jit(solution)/shard_map/all_to_all | solution.py:458
  36.0 0.8 %copy-start.5 = (bf16[480,320]{1,0:T(8,128)(2,1)}, bf16[480,320]{1,0:T(8,128)(2,1)S(1)}, u32[]{:S(2)}) copy-start(bf16[480,320]{1,0:T(8,128)(2,1)S(1)} %collective-permute-done.before_hbm) | copy-start | bytes 921604
  36.0 0.9 %copy-start.6 = (bf16[480,320]{1,0:T(8,128)(2,1)}, bf16[480,320]{1,0:T(8,128)(2,1)S(1)}, u32[]{:S(2)}) copy-start(bf16[480,320]{1,0:T(8,128)(2,1)S(1)} %collective-permute-done.1.after_hbm) | copy-start | bytes 921604
  48.5 8.1 %collective-permute-start.2 = (bf16[160,320]{1,0:T(8,128)(2,1)S(1)}, bf16[160,320]{1,0:T(8,128)(2,1)S(1)}, u32[]{:S(2)}, u32[]{:S(2)}) collective-permute-start(bf16[160,320]{1,0:T(8,128)(2,1)S(1)} %gather_sum.1.grad_ref), channel_id=1, source_target_pairs={{0,2},{2,4},{4,6},{1,3},{3,5},{5,7},{8,10},{10,12},{12,14},{9,11},... | collective-permute-start | bytes 307208 | tf_op jit(solution)/shard_map/ppermute | solution.py:435
  51.3 6.8 %collective-permute-start.3 = (bf16[160,320]{1,0:T(8,128)(2,1)S(1)}, bf16[160,320]{1,0:T(8,128)(2,1)S(1)}, u32[]{:S(2)}, u32[]{:S(2)}) collective-permute-start(bf16[160,320]{1,0:T(8,128)(2,1)S(1)} %gather_sum.1.grad_ref), channel_id=1, source_target_pairs={{2,0},{4,2},{6,4},{3,1},{5,3},{7,5},{10,8},{12,10},{14,12},{11,9},... | collective-permute-start | bytes 307208 | tf_op jit(solution)/shard_map/ppermute | solution.py:436
